TPU v7x, 128 devices: a whole 4x4x4 slice. The times are simulated.
128 devices in a mesh: section: 4 (over x), tensor: 32 (over z, y, core).
Axes of the slice: x: 4, y: 4, z: 4, core: 2. Of those that a mesh axis runs over, the one named last changes fastest.
Arguments:
- inputs: bfloat16 [4, 128, 4096], P(None, None, 'tensor'), may hold values from -6 to 6
- grad_out: bfloat16 [4, 128, 4096], P(None, None, 'tensor'), may hold values from -6 to 6
- tenants: int32 [4], replicated, may hold values from 0 to 3, each once
- base_weight: bfloat16 [4, 4096, 4096], P('section', None, 'tensor'), may hold values from -0.09375 to 0.09375
- adapter_a: bfloat16 [4, 4, 16, 4096], P('section'), may hold values from -0.09375 to 0.09375
- adapter_b: bfloat16 [4, 4, 16, 4096], P('section', None, None, 'tensor'), may hold values from -1.5 to 1.5
- magnitude: float32 [4, 4, 4096], P('section', None, 'tensor'), may hold values from 0.5 to 1.5
Outputs:
- grad_a: float32 [4, 4, 16, 4096], P('section', None, None, 'tensor')
- grad_b: float32 [4, 4, 16, 4096], P('section', None, None, 'tensor')
- grad_magnitude: float32 [4, 4, 4096], P('section', None, 'tensor')
Inputs may be any that keep to these rules, and one draw needn't show every extreme that they name: `tenants`: every tenant serves exactly one micro-batch.
All inputs are finite; a program needn't handle non-finite values.
Results may differ from a plain program's by a relative error of at most 0.008.
Values may be sent and summed in bfloat16 or wider, within the bound.
A program may use at most 64 MiB of HBM per device.

v0:
```python
import jax
import jax.numpy as jnp
from jax import lax
from jax.sharding import PartitionSpec as P


def passed_along(shard, axis, by):
    count = lax.axis_size(axis)
    pairs = [(i, i + by) for i in range(count) if 0 <= i + by < count]
    return lax.ppermute(shard, axis, pairs)


def column_norms(w_base, a_all, b_all):
    wide = w_base.astype(jnp.float32)
    base_sq = jnp.sum(wide * wide, axis=0)
    cross = jnp.einsum("trd,dc->trc", a_all, w_base, preferred_element_type=jnp.float32)
    gram = jnp.einsum("trd,tsd->trs", a_all, a_all, preferred_element_type=jnp.float32)
    b_wide = b_all.astype(jnp.float32)
    quad = jnp.einsum("trs,tsc->trc", gram, b_wide, precision=lax.Precision.HIGHEST)
    total = base_sq[None, :] + jnp.sum(b_wide * (2.0 * cross + quad), axis=1)
    return jnp.sqrt(total + 1e-06)


def contract(left, right, left_dim, right_dim, precision=None):
    return lax.dot_general(
        left,
        right,
        (((left_dim,), (right_dim,)), ((), ())),
        precision=precision,
        preferred_element_type=jnp.float32,
    )


def pick(array, index):
    return lax.dynamic_index_in_dim(array, index, 0, keepdims=False)


def place(array, value, index):
    return lax.dynamic_update_index_in_dim(array, value, index, 0)


def store_when(array, value, index, active):
    return place(array, jnp.where(active, value, pick(array, index)), index)


def local(inputs, grad_out, tenants, base_weight, adapter_a, adapter_b, magnitude):
    sections = lax.axis_size("section")
    section = lax.axis_index("section")
    micro, tokens_mb, cols = inputs.shape
    start = lax.axis_index("tensor") * cols
    tenant_count, rank, width = (adapter_a.shape[1], adapter_a.shape[2], adapter_a.shape[3])
    highest = lax.Precision.HIGHEST
    w_base = base_weight[0]
    a_all = adapter_a[0]
    b_all = adapter_b[0]
    norms = column_norms(w_base, a_all, b_all)
    scales = magnitude[0] / norms
    blank = jnp.zeros((tokens_mb, cols), jnp.bfloat16)
    ticks = sections + micro - 1

    def forward_products(tenant, whole):
        wide = whole.astype(jnp.float32)
        root = jnp.sqrt(jnp.mean(wide * wide, axis=1, keepdims=True) + 1e-05)
        normed = (wide / root).astype(jnp.bfloat16)
        lowrank = contract(normed, pick(a_all, tenant), 1, 1).astype(jnp.bfloat16)
        branch = jnp.dot(normed, w_base, preferred_element_type=jnp.float32)
        branch = branch + jnp.dot(lowrank, pick(b_all, tenant), preferred_element_type=jnp.float32)
        return (lowrank, branch)

    def forward_tick(tick, carry):
        incoming, stores_now = carry
        saved_x, saved_u, saved_z = stores_now
        slot = tick - section
        active = (slot >= 0) & (slot < micro)
        safe_slot = jnp.clip(slot, 0, micro - 1)
        tenant = pick(tenants, safe_slot)
        own = jnp.where(section == 0, pick(inputs, safe_slot), incoming)
        whole = lax.all_gather(own, "tensor", axis=1, tiled=True)
        lowrank, branch = lax.cond(
            active,
            lambda: forward_products(tenant, whole),
            lambda: (
                jnp.zeros((tokens_mb, rank), jnp.bfloat16),
                jnp.zeros((tokens_mb, cols), jnp.float32),
            ),
        )
        result = (own.astype(jnp.float32) + pick(scales, tenant)[None, :] * branch).astype(
            jnp.bfloat16
        )
        result = jnp.where(active, result, blank)
        stores_now = (
            store_when(saved_x, whole, safe_slot, active),
            store_when(saved_u, lowrank, safe_slot, active),
            store_when(saved_z, branch, safe_slot, active),
        )
        return (passed_along(result, "section", 1), stores_now)

    stores = (
        jnp.zeros((micro, tokens_mb, width), jnp.bfloat16),
        jnp.zeros((micro, tokens_mb, rank), jnp.bfloat16),
        jnp.zeros((micro, tokens_mb, cols), jnp.float32),
    )
    arrived, stores = lax.fori_loop(0, ticks, forward_tick, (blank, stores))
    saved_x, saved_u, saved_z = stores

    def backward_products(tenant, upstream, lowrank):
        grad_branch = (upstream * pick(scales, tenant)[None, :]).astype(jnp.bfloat16)
        grad_b = contract(lowrank, grad_branch, 0, 0)
        rank_part = contract(grad_branch, pick(b_all, tenant), 1, 1)
        partial_value = contract(grad_branch, w_base, 1, 1)
        partial_value = partial_value + jnp.dot(
            rank_part, pick(a_all, tenant).astype(jnp.float32), precision=highest
        )
        return (grad_b, rank_part, partial_value)

    def backward_tick(tick, carry):
        incoming, accum_now = carry
        total_a, total_b, total_m = accum_now
        slot = tick - (sections - 1 - section)
        active = (slot >= 0) & (slot < micro)
        safe_slot = jnp.clip(slot, 0, micro - 1)
        tenant = pick(tenants, safe_slot)
        upstream = jnp.where(section == sections - 1, pick(grad_out, safe_slot), incoming).astype(
            jnp.float32
        )
        wide = pick(saved_x, safe_slot).astype(jnp.float32)
        root = jnp.sqrt(jnp.mean(wide * wide, axis=1, keepdims=True) + 1e-05)
        normed = (wide / root).astype(jnp.bfloat16)
        x_own = lax.dynamic_slice_in_dim(wide, start, cols, 1)
        lowrank = pick(saved_u, safe_slot)
        branch = pick(saved_z, safe_slot)
        grad_mag = jnp.sum(upstream * branch, axis=0) / pick(norms, tenant)
        grad_b, rank_part, partial_value = lax.cond(
            active,
            lambda: backward_products(tenant, upstream, lowrank),
            lambda: (
                jnp.zeros((rank, cols), jnp.float32),
                jnp.zeros((tokens_mb, rank), jnp.float32),
                jnp.zeros((tokens_mb, width), jnp.float32),
            ),
        )
        grad_h = lax.psum_scatter(partial_value, "tensor", scatter_dimension=1, tiled=True)
        row_dot = lax.psum(jnp.sum(grad_h * x_own, axis=1, keepdims=True), "tensor")
        grad_in = (upstream + (grad_h - x_own * row_dot / (width * root * root)) / root).astype(
            jnp.bfloat16
        )
        grad_in = jnp.where(active, grad_in, blank)
        rank_sum = lax.psum(rank_part, "tensor")
        normed_own = lax.dynamic_slice_in_dim(normed, start, cols, 1).astype(jnp.float32)
        grad_a = contract(rank_sum, normed_own, 0, 0, highest)
        gate = jnp.where(active, 1.0, 0.0).astype(jnp.float32)
        total_a = place(total_a, pick(total_a, tenant) + gate * grad_a, tenant)
        total_b = place(total_b, pick(total_b, tenant) + gate * grad_b, tenant)
        total_m = place(total_m, pick(total_m, tenant) + gate * grad_mag, tenant)
        return (passed_along(grad_in, "section", -1), (total_a, total_b, total_m))

    accum = (
        jnp.zeros((tenant_count, rank, cols), jnp.float32),
        jnp.zeros((tenant_count, rank, cols), jnp.float32),
        jnp.zeros((tenant_count, cols), jnp.float32),
    )
    returned, accum = lax.fori_loop(0, ticks, backward_tick, (blank, accum))
    total_a, total_b, total_m = accum
    squares = jnp.stack(
        [
            jnp.sum(total_a * total_a, axis=(1, 2)),
            jnp.sum(total_b * total_b, axis=(1, 2)),
            jnp.sum(total_m * total_m, axis=1),
        ]
    )
    squares = lax.psum(squares, ("section", "tensor"))
    count_pair = sections * rank * width
    count_single = sections * width
    out_a = total_a / jnp.sqrt(squares[0] / count_pair + 1e-06)[:, None, None]
    out_b = total_b / jnp.sqrt(squares[1] / count_pair + 1e-06)[:, None, None]
    out_m = total_m / jnp.sqrt(squares[2] / count_single + 1e-06)[:, None]
    return (out_a[None], out_b[None], out_m[None])


def solution(mesh):
    return jax.shard_map(
        local,
        mesh=mesh,
        in_specs=(
            P(None, None, "tensor"),
            P(None, None, "tensor"),
            P(),
            P("section", None, "tensor"),
            P("section", None, None, None),
            P("section", None, None, "tensor"),
            P("section", None, "tensor"),
        ),
        out_specs=(
            P("section", None, None, "tensor"),
            P("section", None, None, "tensor"),
            P("section", None, "tensor"),
        ),
        check_vma=False,
    )
```

profile of v0, /device:TPU:0, one launch (start us, length us, event | category | flops | bytes accessed | tf_op | source)
XLA Modules:
  0.0 1624.0 jit_solution(3132108223348965906)
XLA Ops:
  15.8 412.3 %while.41 = (s32[]{:T(128)}, bf16[128,128]{1,0:T(8,128)(2,1)S(1)}, bf16[4,128,4096]{2,1,0:T(8,128)(2,1)}, bf16[4,128,16]{1,2,0:T(8,128)(2,1)}, f32[4,128,128]{2,...) while((s32[]{:T(128)}, bf16[128,128]{1,0:T(8,128)(2,1)S(1)}, ...), condition=%wide.region_6.7_spmd, body=%wide.region_2.6_spmd.sunk | while | flops 155324544 | bytes 15962108 | solution.py:103
  22.8 42.2 %all-gather.2.cloned.1.call-done = bf16[128,4096]{1,0:T(8,128)(2,1)} async-done(((bf16[128,128]{1,0:T(8,128)(2,1)}), bf16[128,4096]{1,0:T(8,128)(2,1)}) %all-gather.2.cloned.1.call-update) | async-done | bytes 1048592 | tf_op jit(solution)/shard_map/while/body/eval_jaxpr/all_gather | solution.py:78
  65.0 8.0 conditional.4
  85.1 36.5 %all-gather.2.cloned.1.call-done = bf16[128,4096]{1,0:T(8,128)(2,1)} async-done(((bf16[128,128]{1,0:T(8,128)(2,1)}), bf16[128,4096]{1,0:T(8,128)(2,1)}) %all-gather.2.cloned.1.call-update) | async-done | bytes 1048592 | tf_op jit(solution)/shard_map/while/body/eval_jaxpr/all_gather | solution.py:78
  121.6 8.0 conditional.4
  143.9 36.5 %all-gather.2.cloned.1.call-done = bf16[128,4096]{1,0:T(8,128)(2,1)} async-done(((bf16[128,128]{1,0:T(8,128)(2,1)}), bf16[128,4096]{1,0:T(8,128)(2,1)}) %all-gather.2.cloned.1.call-update) | async-done | bytes 1048592 | tf_op jit(solution)/shard_map/while/body/eval_jaxpr/all_gather | solution.py:78
  180.4 8.0 conditional.4
  202.7 37.3 %all-gather.2.cloned.1.call-done = bf16[128,4096]{1,0:T(8,128)(2,1)} async-done(((bf16[128,128]{1,0:T(8,128)(2,1)}), bf16[128,4096]{1,0:T(8,128)(2,1)}) %all-gather.2.cloned.1.call-update) | async-done | bytes 1048592 | tf_op jit(solution)/shard_map/while/body/eval_jaxpr/all_gather | solution.py:78
  240.0 8.0 conditional.4
  262.2 38.4 %all-gather.2.cloned.1.call-done = bf16[128,4096]{1,0:T(8,128)(2,1)} async-done(((bf16[128,128]{1,0:T(8,128)(2,1)}), bf16[128,4096]{1,0:T(8,128)(2,1)}) %all-gather.2.cloned.1.call-update) | async-done | bytes 1048592 | tf_op jit(solution)/shard_map/while/body/eval_jaxpr/all_gather | solution.py:78
  301.4 10.6 collective-permute-start
  320.9 40.2 %all-gather.2.cloned.1.call-done = bf16[128,4096]{1,0:T(8,128)(2,1)} async-done(((bf16[128,128]{1,0:T(8,128)(2,1)}), bf16[128,4096]{1,0:T(8,128)(2,1)}) %all-gather.2.cloned.1.call-update) | async-done | bytes 1048592 | tf_op jit(solution)/shard_map/while/body/eval_jaxpr/all_gather | solution.py:78
  374.2 47.8 %all-gather.2.cloned.1.call-done = bf16[128,4096]{1,0:T(8,128)(2,1)} async-done(((bf16[128,128]{1,0:T(8,128)(2,1)}), bf16[128,4096]{1,0:T(8,128)(2,1)}) %all-gather.2.cloned.1.call-update) | async-done | bytes 1048592 | tf_op jit(solution)/shard_map/while/body/eval_jaxpr/all_gather | solution.py:78
  428.7 1122.5 %while.42 = (s32[]{:T(128)}, bf16[128,128]{1,0:T(8,128)(2,1)S(1)}, f32[4,16,128]{2,1,0:T(8,128)}, f32[4,16,128]{2,1,0:T(8,128)S(1)}, f32[4,128]{1,0:T(4,128)S(1)...) while((s32[]{:T(128)}, bf16[128,128]{1,0:T(8,128)(2,1)S(1)}, ...), condition=%wide.region_16.17_spmd, body=%wide.region_7.16_spmd.sunk | while | flops 241986176 | bytes 29732976 | solution.py:162
  440.7 84.5 %reduce-scatter.2.cloned.1.call-done = f32[128,128]{1,0:T(8,128)} async-done(((f32[128,4096]{1,0:T(8,128)}), f32[128,128]{1,0:T(8,128)}) %reduce-scatter.2.cloned.1.call-update) | async-done | bytes 65552 | tf_op jit(solution)/shard_map/while/body/eval_jaxpr/reduce_scatter | solution.py:142
  526.2 65.8 %all-reduce.2 = (f32[128]{0:T(128)S(1)}, f32[128,16]{0,1:T(8,128)}) all-reduce(f32[128]{0:T(128)S(1)} %fusion.75, f32[128,16]{0,1:T(8,128)} %get-tuple-element.1006), channel_id=1, replica_groups=mesh['section'=4,'tensor'=32] {'tensor'}, use_global_device_ids=true, to_apply=%region_12.12 | all-reduce | flops 2176 | bytes 17408 | tf_op jit(solution)/shard_map/while/body/eval_jaxpr/psum | solution.py:143
  610.7 74.0 %reduce-scatter.2.cloned.1.call-done = f32[128,128]{1,0:T(8,128)} async-done(((f32[128,4096]{1,0:T(8,128)}), f32[128,128]{1,0:T(8,128)}) %reduce-scatter.2.cloned.1.call-update) | async-done | bytes 65552 | tf_op jit(solution)/shard_map/while/body/eval_jaxpr/reduce_scatter | solution.py:142
  685.6 65.8 %all-reduce.2 = (f32[128]{0:T(128)S(1)}, f32[128,16]{0,1:T(8,128)}) all-reduce(f32[128]{0:T(128)S(1)} %fusion.75, f32[128,16]{0,1:T(8,128)} %get-tuple-element.1006), channel_id=1, replica_groups=mesh['section'=4,'tensor'=32] {'tensor'}, use_global_device_ids=true, to_apply=%region_12.12 | all-reduce | flops 2176 | bytes 17408 | tf_op jit(solution)/shard_map/while/body/eval_jaxpr/psum | solution.py:143
  770.2 73.9 %reduce-scatter.2.cloned.1.call-done = f32[128,128]{1,0:T(8,128)} async-done(((f32[128,4096]{1,0:T(8,128)}), f32[128,128]{1,0:T(8,128)}) %reduce-scatter.2.cloned.1.call-update) | async-done | bytes 65552 | tf_op jit(solution)/shard_map/while/body/eval_jaxpr/reduce_scatter | solution.py:142
  845.0 65.8 %all-reduce.2 = (f32[128]{0:T(128)S(1)}, f32[128,16]{0,1:T(8,128)}) all-reduce(f32[128]{0:T(128)S(1)} %fusion.75, f32[128,16]{0,1:T(8,128)} %get-tuple-element.1006), channel_id=1, replica_groups=mesh['section'=4,'tensor'=32] {'tensor'}, use_global_device_ids=true, to_apply=%region_12.12 | all-reduce | flops 2176 | bytes 17408 | tf_op jit(solution)/shard_map/while/body/eval_jaxpr/psum | solution.py:143
  919.7 7.1 conditional.5
  935.9 67.6 %reduce-scatter.2.cloned.1.call-done = f32[128,128]{1,0:T(8,128)} async-done(((f32[128,4096]{1,0:T(8,128)}), f32[128,128]{1,0:T(8,128)}) %reduce-scatter.2.cloned.1.call-update) | async-done | bytes 65552 | tf_op jit(solution)/shard_map/while/body/eval_jaxpr/reduce_scatter | solution.py:142
  1004.5 65.9 %all-reduce.2 = (f32[128]{0:T(128)S(1)}, f32[128,16]{0,1:T(8,128)}) all-reduce(f32[128]{0:T(128)S(1)} %fusion.75, f32[128,16]{0,1:T(8,128)} %get-tuple-element.1006), channel_id=1, replica_groups=mesh['section'=4,'tensor'=32] {'tensor'}, use_global_device_ids=true, to_apply=%region_12.12 | all-reduce | flops 2176 | bytes 17408 | tf_op jit(solution)/shard_map/while/body/eval_jaxpr/psum | solution.py:143
  1095.4 67.6 %reduce-scatter.2.cloned.1.call-done = f32[128,128]{1,0:T(8,128)} async-done(((f32[128,4096]{1,0:T(8,128)}), f32[128,128]{1,0:T(8,128)}) %reduce-scatter.2.cloned.1.call-update) | async-done | bytes 65552 | tf_op jit(solution)/shard_map/while/body/eval_jaxpr/reduce_scatter | solution.py:142
  1164.0 65.9 %all-reduce.2 = (f32[128]{0:T(128)S(1)}, f32[128,16]{0,1:T(8,128)}) all-reduce(f32[128]{0:T(128)S(1)} %fusion.75, f32[128,16]{0,1:T(8,128)} %get-tuple-element.1006), channel_id=1, replica_groups=mesh['section'=4,'tensor'=32] {'tensor'}, use_global_device_ids=true, to_apply=%region_12.12 | all-reduce | flops 2176 | bytes 17408 | tf_op jit(solution)/shard_map/while/body/eval_jaxpr/psum | solution.py:143
  1238.7 7.1 conditional.5
  1254.9 66.1 %reduce-scatter.2.cloned.1.call-done = f32[128,128]{1,0:T(8,128)} async-done(((f32[128,4096]{1,0:T(8,128)}), f32[128,128]{1,0:T(8,128)}) %reduce-scatter.2.cloned.1.call-update) | async-done | bytes 65552 | tf_op jit(solution)/shard_map/while/body/eval_jaxpr/reduce_scatter | solution.py:142
  1321.9 65.9 %all-reduce.2 = (f32[128]{0:T(128)S(1)}, f32[128,16]{0,1:T(8,128)}) all-reduce(f32[128]{0:T(128)S(1)} %fusion.75, f32[128,16]{0,1:T(8,128)} %get-tuple-element.1006), channel_id=1, replica_groups=mesh['section'=4,'tensor'=32] {'tensor'}, use_global_device_ids=true, to_apply=%region_12.12 | all-reduce | flops 2176 | bytes 17408 | tf_op jit(solution)/shard_map/while/body/eval_jaxpr/psum | solution.py:143
  1396.6 7.1 conditional.5
  1412.9 64.7 %reduce-scatter.2.cloned.1.call-done = f32[128,128]{1,0:T(8,128)} async-done(((f32[128,4096]{1,0:T(8,128)}), f32[128,128]{1,0:T(8,128)}) %reduce-scatter.2.cloned.1.call-update) | async-done | bytes 65552 | tf_op jit(solution)/shard_map/while/body/eval_jaxpr/reduce_scatter | solution.py:142
  1478.6 65.9 %all-reduce.2 = (f32[128]{0:T(128)S(1)}, f32[128,16]{0,1:T(8,128)}) all-reduce(f32[128]{0:T(128)S(1)} %fusion.75, f32[128,16]{0,1:T(8,128)} %get-tuple-element.1006), channel_id=1, replica_groups=mesh['section'=4,'tensor'=32] {'tensor'}, use_global_device_ids=true, to_apply=%region_12.12 | all-reduce | flops 2176 | bytes 17408 | tf_op jit(solution)/shard_map/while/body/eval_jaxpr/psum | solution.py:143
  1552.3 63.0 %psum.33 = f32[3,4]{1,0:T(4,128)S(1)} all-reduce(f32[3,4]{1,0:T(4,128)S(1)} %pad_maximum_fusion), channel_id=1, replica_groups=mesh['section'=4,'tensor'=32] {'section','tensor'}, use_global_device_ids=true, to_apply=%region_20.21 | all-reduce | flops 12 | bytes 96 | tf_op jit(solution)/shard_map/psum | solution.py:171
  (331 shorter events, 271.0 us)
Async XLA Ops:
  15.8 49.2 %all-gather.2.cloned.1.call-start = ((), (), s32[]{:S(2)}) async-start(), calls=%async_computation.1 | async-start | bytes 1081344 | tf_op jit(solution)/shard_map/while/body/eval_jaxpr/all_gather | solution.py:78
  65.0 8.0 copy-start.2
  73.0 5.1 collective-permute-start
  78.1 43.6 %all-gather.2.cloned.1.call-start = ((), (), s32[]{:S(2)}) async-start(), calls=%async_computation.1 | async-start | bytes 1081344 | tf_op jit(solution)/shard_map/while/body/eval_jaxpr/all_gather | solution.py:78
  121.6 8.0 copy-start.2
  129.7 7.2 collective-permute-start
  136.9 43.6 %all-gather.2.cloned.1.call-start = ((), (), s32[]{:S(2)}) async-start(), calls=%async_computation.1 | async-start | bytes 1081344 | tf_op jit(solution)/shard_map/while/body/eval_jaxpr/all_gather | solution.py:78
  180.4 8.0 copy-start.2
  188.5 7.1 collective-permute-start
  195.6 44.4 %all-gather.2.cloned.1.call-start = ((), (), s32[]{:S(2)}) async-start(), calls=%async_computation.1 | async-start | bytes 1081344 | tf_op jit(solution)/shard_map/while/body/eval_jaxpr/all_gather | solution.py:78
  240.0 8.0 copy-start.2
  248.0 7.1 collective-permute-start
  255.1 45.4 %all-gather.2.cloned.1.call-start = ((), (), s32[]{:S(2)}) async-start(), calls=%async_computation.1 | async-start | bytes 1081344 | tf_op jit(solution)/shard_map/while/body/eval_jaxpr/all_gather | solution.py:78
  301.4 12.5 collective-permute-start
  313.9 47.3 %all-gather.2.cloned.1.call-start = ((), (), s32[]{:S(2)}) async-start(), calls=%async_computation.1 | async-start | bytes 1081344 | tf_op jit(solution)/shard_map/while/body/eval_jaxpr/all_gather | solution.py:78
  361.9 5.2 collective-permute-start
  367.2 54.9 %all-gather.2.cloned.1.call-start = ((), (), s32[]{:S(2)}) async-start(), calls=%async_computation.1 | async-start | bytes 1081344 | tf_op jit(solution)/shard_map/while/body/eval_jaxpr/all_gather | solution.py:78
  422.8 5.2 collective-permute-start
  428.7 96.5 %reduce-scatter.2.cloned.1.call-start = ((), (), s32[]{:S(2)}) async-start(), calls=%async_computation.2 | async-start | bytes 2162688 | tf_op jit(solution)/shard_map/while/body/eval_jaxpr/reduce_scatter | solution.py:142
  592.9 5.8 collective-permute-start.1
  598.8 85.9 %reduce-scatter.2.cloned.1.call-start = ((), (), s32[]{:S(2)}) async-start(), calls=%async_computation.2 | async-start | bytes 2162688 | tf_op jit(solution)/shard_map/while/body/eval_jaxpr/reduce_scatter | solution.py:142
  752.4 5.8 collective-permute-start.1
  758.2 85.9 %reduce-scatter.2.cloned.1.call-start = ((), (), s32[]{:S(2)}) async-start(), calls=%async_computation.2 | async-start | bytes 2162688 | tf_op jit(solution)/shard_map/while/body/eval_jaxpr/reduce_scatter | solution.py:142
  911.8 5.8 collective-permute-start.1
  917.6 85.9 %reduce-scatter.2.cloned.1.call-start = ((), (), s32[]{:S(2)}) async-start(), calls=%async_computation.2 | async-start | bytes 2162688 | tf_op jit(solution)/shard_map/while/body/eval_jaxpr/reduce_scatter | solution.py:142
  1071.3 5.8 collective-permute-start.1
  1077.1 85.9 %reduce-scatter.2.cloned.1.call-start = ((), (), s32[]{:S(2)}) async-start(), calls=%async_computation.2 | async-start | bytes 2162688 | tf_op jit(solution)/shard_map/while/body/eval_jaxpr/reduce_scatter | solution.py:142
  1230.8 5.8 collective-permute-start.1
  1236.6 84.4 %reduce-scatter.2.cloned.1.call-start = ((), (), s32[]{:S(2)}) async-start(), calls=%async_computation.2 | async-start | bytes 2162688 | tf_op jit(solution)/shard_map/while/body/eval_jaxpr/reduce_scatter | solution.py:142
  1388.8 5.8 collective-permute-start.1
  1394.6 83.0 %reduce-scatter.2.cloned.1.call-start = ((), (), s32[]{:S(2)}) async-start(), calls=%async_computation.2 | async-start | bytes 2162688 | tf_op jit(solution)/shard_map/while/body/eval_jaxpr/reduce_scatter | solution.py:142
  1545.4 5.8 collective-permute-start.1
  (12 other events, 20.9 us)
Sparse Core Ops, SparseCore 0:
  19.3 45.5 all-gather.1
  81.6 39.9 all-gather.1
  140.4 39.9 all-gather.1
  198.9 41.0 all-gather.1
  258.4 42.1 all-gather.1
  317.1 43.9 all-gather.1
  370.8 51.2 all-gather.1
  433.1 92.0 reduce-scatter.1
  603.1 81.5 reduce-scatter.1
  762.6 81.4 reduce-scatter.1
  928.3 75.2 reduce-scatter.1
  1087.8 75.1 reduce-scatter.1
  1247.3 73.6 reduce-scatter.1
  1405.2 72.3 reduce-scatter.1
where the time goes:
time: 1630 us; the launch traced here: 1620 us
  waiting for transfers between devices  797 us (49%)
  blocking collectives  524 us (32%)
  other arithmetic  108 us (7%)
  local copies, waits for them, and re-layouts  56.8 us (3%)
  matrix products  47.7 us (3%)
  loops' own time  38.8 us (2%)
  starting transfers between devices  37.9 us (2%)
    reduce_scatter x7, waiting for transfers between devices, backward_tick(): lax.psum_scatter(partial_value, 'tensor', scatter_dimension=1, tiled=True)  498 us
    psum x7, blocking collectives, backward_tick(): row_dot = lax.psum(jnp.sum(grad_h * x_own, axis=1, keepdims=True), 'tensor')  461 us
    all_gather x7, waiting for transfers between devices, forward_tick(): whole = lax.all_gather(own, 'tensor', axis=1, tiled=True)  279 us
    psum x1, blocking collectives, local(): squares = lax.psum(squares, ('section', 'tensor'))  63 us
    ppermute x14, starting transfers between devices, passed_along(): return lax.ppermute(shard, axis, pairs)  37.8 us
  transfers between devices with their start and end apart: 28, of which 21 were waited for; matrix products, arithmetic and copies ran while one was open for 6% of the time, Pallas kernels for 0%

commit v1 on v0

v1 whole, which is shorter than its diff:
```python
import jax
import jax.numpy as jnp
from jax import lax
from jax.experimental import pallas as pl
from jax.experimental.pallas import tpu as pltpu
from jax.sharding import PartitionSpec as P

MESH = pl.DeviceIdType.MESH
F32 = jnp.float32
BF16 = jnp.bfloat16

L = 4
TOK = 128
D = 4096
R = 16
COLS = 128
CHIPS = 16
BLK = TOK + R
EXT = 32
RSB = TOK + EXT
HALF = D // 2
WCH = 8
WROWS = HALF // WCH

OFFSETS = [(dz, dy) for dz in range(4) for dy in range(4)]


def hops(r):
    dz, dy = OFFSETS[r]
    return min(dz, 4 - dz) + min(dy, 4 - dy)


NEAR = sorted(range(1, CHIPS), key=hops)
FAR = NEAR[::-1]


def inverse(r):
    dz, dy = OFFSETS[r]
    return ((4 - dz) % 4) * 4 + (4 - dy) % 4


def dot(a, b, ca, cb, precision=None):
    return lax.dot_general(
        a, b, (((ca,), (cb,)), ((), ())), precision=precision, preferred_element_type=F32
    )


def split3(v):
    hi = v.astype(BF16)
    rest = v - hi.astype(F32)
    mid = rest.astype(BF16)
    low = (rest - mid.astype(F32)).astype(BF16)
    return jnp.concatenate([hi, mid, low], axis=0)


def fold3(v):
    return v[0:R] + v[R : 2 * R] + v[2 * R : 3 * R]


def kernel(
    ten_ref, x_ref, g_ref, w_hbm, a_hbm, b_ref, m_ref,
    oa_ref, ob_ref, om_ref,
    w_buf, a_own, sm_src, mg_src, sm_buf, mg_buf, xg, cur,
    sv_branch, sv_low, sv_root, sv_norm, sv_scale,
    cs_src, cs_dst, ce_src, ce_dst, rs_src, rs_dst, ex_src, ex_dst,
    res, od_src, od_dst,
    loc_sem, w_send, w_recv, sm_send, sm_recv, mg_send, mg_recv,
    ag_send, ag_recv, cf_send, cf_recv,
    cs_send, cs_recv, ce_send, ce_recv, rs_send, rs_recv, ex_send, ex_recv,
    od_send, od_recv,
):
    s = lax.axis_index("section")
    t = lax.axis_index("tensor")
    z = t // 8
    y = (t // 2) % 4
    c = t % 2

    def plane(r):
        dz, dy = OFFSETS[r]
        return (s, ((z + dz) % 4) * 8 + ((y + dy) % 4) * 2 + c)

    def source(r):
        dz, dy = OFFSETS[r]
        return ((z + 4 - dz) % 4) * 4 + (y + 4 - dy) % 4

    partner = (s, t + 1 - 2 * c)

    def section(d):
        return ((s + d) % 4, t)

    def remote(src, dst, send, recv, device):
        return pltpu.make_async_remote_copy(
            src_ref=src, dst_ref=dst, send_sem=send, recv_sem=recv,
            device_id=device, device_id_type=MESH,
        )

    def w_copy(layer, way, j, device, from_hbm=False):
        rows = pl.ds(way * HALF + j * WROWS, WROWS)
        src = w_hbm.at[0, rows] if from_hbm else w_buf.at[layer, rows]
        return remote(
            src, w_buf.at[layer, rows], w_send.at[layer, way, j], w_recv.at[layer, way, j], device
        )

    def sm_copy(d):
        return remote(sm_src.at[d], sm_buf.at[s], sm_send.at[d], sm_recv.at[d], section(d))

    def mg_copy(d):
        return remote(mg_src.at[d], mg_buf.at[s], mg_send.at[d], mg_recv.at[d], section(d))

    def ag_copy(l, r):
        return remote(xg.at[l, 0, c], xg.at[l, r, c], ag_send.at[l, r], ag_recv.at[l, r], plane(r))

    def cf_copy(l, r, core):
        return remote(
            xg.at[l, r, core], xg.at[l, r, core], cf_send.at[l, r], cf_recv.at[l, r], partner
        )

    def cs_copy(l, r):
        return remote(
            cs_src.at[l, r], cs_dst.at[l, r], cs_send.at[l, r], cs_recv.at[l, r], partner
        )

    def ce_copy(l):
        return remote(ce_src.at[l], ce_dst.at[l], ce_send.at[l], ce_recv.at[l], partner)

    def rs_copy(l, r):
        return remote(
            rs_src.at[l, r], rs_dst.at[l, r], rs_send.at[l, r], rs_recv.at[l, r], plane(r)
        )

    def ex_copy(r):
        return remote(ex_src, ex_dst.at[r], ex_send.at[r], ex_recv.at[r], plane(r))

    def od_copy(d):
        return remote(
            od_src.at[(s + d) % 4], od_dst.at[s], od_send.at[d], od_recv.at[d], section(d)
        )

    own_w = pltpu.make_async_copy(w_hbm.at[0], w_buf.at[s], loc_sem.at[0])
    own_w.start()
    own_a = pltpu.make_async_copy(
        a_hbm.at[0, :, :, pl.ds(pl.multiple_of(t * COLS, COLS), COLS)], a_own, loc_sem.at[1]
    )
    own_a.start()
    for j in range(WCH):
        w_copy(s, 0, j, section(1), True).start()
        w_copy(s, 1, j, section(3), True).start()
    own_a.wait()
    for d in range(4):
        tenant = ten_ref[(s + d) % 4]
        pair = jnp.concatenate([a_own[tenant], b_ref[0, tenant]], axis=0)
        mag = jnp.broadcast_to(m_ref[0, pl.ds(tenant, 1), :], (8, COLS))
        if d == 0:
            sm_buf[s] = pair
            mg_buf[s] = mag
        else:
            sm_src[d] = pair
            mg_src[d] = mag
            sm_copy(d).start()
            mg_copy(d).start()
    cur[...] = x_ref[s]
    for d in range(1, 4):
        sm_copy(d).wait_recv()
        mg_copy(d).wait_recv()

    def send_block(l):
        xg[l, 0, c] = jnp.concatenate([cur[...], sm_buf[l, 0:R]], axis=0)
        for r in FAR:
            ag_copy(l, r).start()
        cf_copy(l, 0, c).start()

    send_block(0)

    def hop(h):
        def body(j, _):
            a_layer, b_layer = (s + 4 - h) % 4, (s + h) % 4
            w_copy(a_layer, 0, j, section(1)).wait_recv()
            if h < 3:
                w_copy(a_layer, 0, j, section(1)).start()
            w_copy(b_layer, 1, j, section(3)).wait_recv()
            if h < 3:
                w_copy(b_layer, 1, j, section(3)).start()
            return 0

        lax.fori_loop(0, WCH, body, 0)

    for h in (1, 2, 3):
        hop(h)
    own_w.wait()

    def forward(l, _):
        @pl.when(l > 0)
        def _():
            send_block(l)

        def squares(i, total):
            rows = w_buf[l, pl.ds(pl.multiple_of(i * 256, 256), 256), :].astype(F32)
            return total + jnp.sum((rows * rows).reshape(32, 8, COLS), axis=0)

        base_sq = jnp.sum(
            lax.fori_loop(0, 16, squares, jnp.zeros((8, COLS), F32)), axis=0, keepdims=True
        )

        acc = jnp.zeros((BLK, COLS), F32)
        low_acc = jnp.zeros((BLK, R), F32)
        ssq = jnp.zeros((TOK, COLS), F32)

        def use(r, acc, low_acc, ssq):
            cf_copy(l, r, 1 - c).wait_recv()
            both = jnp.concatenate([xg[l, r, 0], xg[l, r, 1]], axis=1)
            rows = w_buf[l, pl.ds(pl.multiple_of(source(r) * 256, 256), 256), :]
            acc = acc + dot(both, rows, 1, 0)
            low_acc = low_acc + dot(both, both[TOK:BLK], 1, 1)
            wide = both[0:TOK].astype(F32)
            wide = wide * wide
            return acc, low_acc, ssq + wide[:, 0:COLS] + wide[:, COLS:]

        before = 0
        for r in NEAR:
            ag_copy(l, r).wait_recv()
            cf_copy(l, r, c).start()
            acc, low_acc, ssq = use(before, acc, low_acc, ssq)
            before = r
        acc, low_acc, ssq = use(before, acc, low_acc, ssq)

        mean = jnp.sum(ssq, axis=1, keepdims=True) * (1.0 / D)
        root = jnp.sqrt(mean + 1e-05)
        inv = 1.0 / root
        b_l = sm_buf[l, R : 2 * R]
        b_wide = b_l.astype(F32)
        low = (low_acc[0:TOK] * inv).astype(BF16)
        branch = acc[0:TOK] * inv + dot(low, b_l, 1, 0)
        quad = dot(low_acc[TOK:BLK], b_wide, 1, 0, lax.Precision.HIGHEST)
        cross = acc[TOK:BLK]
        total = base_sq + jnp.sum(b_wide * (2.0 * cross + quad), axis=0, keepdims=True)
        norm = jnp.sqrt(total + 1e-06)
        scale = mg_buf[l, 0:1] / norm
        sv_branch[l] = branch
        sv_low[l] = low
        sv_root[l] = jnp.broadcast_to(root, (TOK, COLS))
        sv_norm[l] = jnp.broadcast_to(norm, (8, COLS))
        sv_scale[l] = jnp.broadcast_to(scale, (8, COLS))
        cur[...] = (cur[...].astype(F32) + scale * branch).astype(BF16)
        return 0

    lax.fori_loop(0, L, forward, 0)

    cur[...] = g_ref[s]

    def local_grads(l):
        up = cur[...].astype(F32)
        branch = sv_branch[l]
        grad_branch = (up * sv_scale[l, 0:1]).astype(BF16)
        gm = jnp.sum(up * branch, axis=0, keepdims=True) / sv_norm[l, 0:1]
        gb = dot(sv_low[l], grad_branch, 0, 0)
        rank_t = dot(sm_buf[l, R : 2 * R], grad_branch, 1, 1)
        res[l, R : 2 * R] = gb
        res[l, 2 * R : 2 * R + 8] = jnp.broadcast_to(gm, (8, COLS))
        return up, branch, grad_branch, rank_t

    def adapter_grad(l, rank_sum):
        normed = (xg[l, 0, c, 0:TOK].astype(F32) / sv_root[l]).astype(BF16)
        ga = fold3(dot(split3(rank_sum), normed, 1, 0))
        res[l, 0:R] = ga
        return ga

    def backward(i, _):
        l = L - 1 - i
        up, branch, grad_branch, rank_t = local_grads(l)
        root = sv_root[l]
        prod = grad_branch.astype(F32) * branch * root
        row = jnp.sum(prod.T, axis=0, keepdims=True)
        ce_src[l] = jnp.concatenate([rank_t, jnp.broadcast_to(row, (8, TOK))], axis=0)
        ce_copy(l).start()
        rank = rank_t.T
        rank_hi = rank.astype(BF16)
        rank_lo = (rank - rank_hi.astype(F32)).astype(BF16)
        rank_two = jnp.concatenate([rank_hi, rank_lo], axis=1)

        def part(r, core):
            dest = source(inverse(r))
            start = pl.multiple_of(dest * 256 + core * COLS, COLS)
            rows = w_buf[l, pl.ds(start, COLS), :]
            a_d = xg[l, inverse(r), core, TOK:BLK]
            return dot(grad_branch, rows, 1, 1) + dot(
                rank_two, jnp.concatenate([a_d, a_d], axis=0), 1, 0
            )

        order = FAR + [0]
        for r in order:
            cs_src[l, r] = part(r, 1 - c).astype(BF16)
            cs_copy(l, r).start()
        ce_copy(l).wait_recv()
        ext = ce_src[l] + ce_dst[l]
        row = ext[R : R + 8]
        row_hi = row.astype(BF16).astype(F32)
        ext = jnp.concatenate([ext[0:R], row_hi, row - row_hi], axis=0)
        ext_b = ext.astype(BF16)
        own = None
        for r in order:
            mine = part(r, c)
            cs_copy(l, r).wait_recv()
            mine = mine + cs_dst[l, r].astype(F32)
            if r:
                rs_src[l, r, 0:TOK] = mine.astype(BF16)
                rs_src[l, r, TOK:RSB] = ext_b
                rs_copy(l, r).start()
            else:
                own = mine
        total = jnp.concatenate([own, ext], axis=0)
        for r in NEAR:
            rs_copy(l, r).wait_recv()
            total = total + rs_dst[l, r].astype(F32)
        grad_h = total[0:TOK]
        rank_sum = total[TOK : TOK + R]
        row = total[TOK + R : TOK + R + 1] + total[TOK + R + 8 : TOK + R + 9]
        row_dot = jnp.broadcast_to(row, (TOK, TOK)).T
        x_own = xg[l, 0, c, 0:TOK].astype(F32)
        inv = 1.0 / root
        cur[...] = (up + (grad_h - x_own * (row_dot * (inv * inv) * (1.0 / D))) * inv).astype(BF16)
        adapter_grad(l, rank_sum)
        return 0

    lax.fori_loop(0, L - 1, backward, 0)

    _, _, _, rank_t = local_grads(0)
    sum_a = jnp.zeros((1, COLS), F32)
    sum_b = jnp.zeros((1, COLS), F32)
    sum_m = jnp.zeros((1, COLS), F32)
    for l in range(L):
        if l:
            ga = res[l, 0:R]
            sum_a = sum_a + jnp.sum(ga * ga, axis=0, keepdims=True)
        gb = res[l, R : 2 * R]
        sum_b = sum_b + jnp.sum(gb * gb, axis=0, keepdims=True)
        gm = res[l, 2 * R : 2 * R + 1]
        sum_m = sum_m + gm * gm
    ce_src[0] = jnp.concatenate(
        [rank_t, sum_a, sum_b, sum_m, jnp.zeros((5, COLS), F32)], axis=0
    )
    ce_copy(0).start()
    ce_copy(0).wait_recv()
    ext = ce_src[0] + ce_dst[0]
    ex_src[...] = ext
    for r in FAR:
        ex_copy(r).start()
    for r in NEAR:
        ex_copy(r).wait_recv()
        ext = ext + ex_dst[r]
    rank_sum = ext[0:R]
    adapter_grad(0, rank_sum)
    inv_row = (1.0 / sv_root[0]).T[0:1]
    rank_parts = split3(rank_sum * inv_row)
    sq = jnp.zeros((R, COLS), F32)
    for r in range(CHIPS):
        for core in range(2):
            ga = fold3(dot(rank_parts, xg[0, r, core, 0:TOK], 1, 0))
            sq = sq + ga * ga

    def norm_of(v, count):
        return 1.0 / jnp.sqrt(jnp.sum(v, axis=1, keepdims=True) * (1.0 / count) + 1e-06)

    by_a = norm_of(ext[R : R + 1] + jnp.sum(sq, axis=0, keepdims=True), L * R * D)
    by_b = norm_of(ext[R + 1 : R + 2], L * R * D)
    by_m = norm_of(ext[R + 2 : R + 3], L * D)
    for l in range(L):
        od_src[l, 0:R] = res[l, 0:R] * by_a
        od_src[l, R : 2 * R] = res[l, R : 2 * R] * by_b
        od_src[l, 2 * R : 2 * R + 8] = res[l, 2 * R : 2 * R + 8] * by_m
    for d in (2, 1, 3):
        od_copy(d).start()
    od_dst[s] = od_src[s]
    for d in (1, 3, 2):
        od_copy(d).wait_recv()
    for tenant in range(4):
        out = jnp.zeros((2 * R + 8, COLS), F32)
        for k in range(4):
            out = jnp.where(ten_ref[k] == tenant, od_dst[k], out)
        oa_ref[0, tenant] = out[0:R]
        ob_ref[0, tenant] = out[R : 2 * R]
        om_ref[0, pl.ds(tenant, 1), :] = out[2 * R : 2 * R + 1]

    def drain_w(j, _):
        for h in range(3):
            w_copy((s + 4 - h) % 4, 0, j, section(1)).wait_send()
            w_copy((s + h) % 4, 1, j, section(3)).wait_send()
        return 0

    lax.fori_loop(0, WCH, drain_w, 0)

    def drain_l(l, _):
        for r in range(CHIPS):
            cf_copy(l, r, c).wait_send()
            if r:
                ag_copy(l, r).wait_send()
        ce_copy(l).wait_send()
        return 0

    lax.fori_loop(0, L, drain_l, 0)

    def drain_b(l, _):
        for r in range(CHIPS):
            cs_copy(l, r).wait_send()
            if r:
                rs_copy(l, r).wait_send()
        return 0

    lax.fori_loop(1, L, drain_b, 0)
    for r in range(1, CHIPS):
        ex_copy(r).wait_send()
    for d in range(1, 4):
        sm_copy(d).wait_send()
        mg_copy(d).wait_send()
        od_copy(d).wait_send()


def local(inputs, grad_out, tenants, base_weight, adapter_a, adapter_b, magnitude):
    vmem = pl.BlockSpec(memory_space=pltpu.VMEM)
    hbm = pl.BlockSpec(memory_space=pl.ANY)
    dma = pltpu.SemaphoreType.DMA
    return pl.pallas_call(
        kernel,
        out_shape=(
            jax.ShapeDtypeStruct((1, 4, R, COLS), F32),
            jax.ShapeDtypeStruct((1, 4, R, COLS), F32),
            jax.ShapeDtypeStruct((1, 4, COLS), F32),
        ),
        in_specs=[pl.BlockSpec(memory_space=pltpu.SMEM), vmem, vmem, hbm, hbm, vmem, vmem],
        out_specs=(vmem, vmem, vmem),
        scratch_shapes=[
            pltpu.VMEM((L, D, COLS), BF16),
            pltpu.VMEM((4, R, COLS), BF16),
            pltpu.VMEM((4, 2 * R, COLS), BF16),
            pltpu.VMEM((4, 8, COLS), F32),
            pltpu.VMEM((4, 2 * R, COLS), BF16),
            pltpu.VMEM((4, 8, COLS), F32),
            pltpu.VMEM((L, CHIPS, 2, BLK, COLS), BF16),
            pltpu.VMEM((TOK, COLS), BF16),
            pltpu.VMEM((L, TOK, COLS), F32),
            pltpu.VMEM((L, TOK, R), BF16),
            pltpu.VMEM((L, TOK, COLS), F32),
            pltpu.VMEM((L, 8, COLS), F32),
            pltpu.VMEM((L, 8, COLS), F32),
            pltpu.VMEM((L, CHIPS, TOK, COLS), BF16),
            pltpu.VMEM((L, CHIPS, TOK, COLS), BF16),
            pltpu.VMEM((L, R + 8, TOK), F32),
            pltpu.VMEM((L, R + 8, TOK), F32),
            pltpu.VMEM((L, CHIPS, RSB, COLS), BF16),
            pltpu.VMEM((L, CHIPS, RSB, COLS), BF16),
            pltpu.VMEM((R + 8, TOK), F32),
            pltpu.VMEM((CHIPS, R + 8, TOK), F32),
            pltpu.VMEM((L, 2 * R + 8, COLS), F32),
            pltpu.VMEM((L, 2 * R + 8, COLS), F32),
            pltpu.VMEM((L, 2 * R + 8, COLS), F32),
            dma((2,)),
            dma((L, 2, WCH)),
            dma((L, 2, WCH)),
            dma((4,)),
            dma((4,)),
            dma((4,)),
            dma((4,)),
            dma((L, CHIPS)),
            dma((L, CHIPS)),
            dma((L, CHIPS)),
            dma((L, CHIPS)),
            dma((L, CHIPS)),
            dma((L, CHIPS)),
            dma((L,)),
            dma((L,)),
            dma((L, CHIPS)),
            dma((L, CHIPS)),
            dma((CHIPS,)),
            dma((CHIPS,)),
            dma((4,)),
            dma((4,)),
        ],
        compiler_params=pltpu.CompilerParams(
            has_side_effects=True, vmem_limit_bytes=48 * 2**20
        ),
    )(tenants, inputs, grad_out, base_weight, adapter_a, adapter_b, magnitude)


def solution(mesh):
    return jax.shard_map(
        local,
        mesh=mesh,
        in_specs=(
            P(None, None, "tensor"),
            P(None, None, "tensor"),
            P(),
            P("section", None, "tensor"),
            P("section", None, None, None),
            P("section", None, None, "tensor"),
            P("section", None, "tensor"),
        ),
        out_specs=(
            P("section", None, None, "tensor"),
            P("section", None, None, "tensor"),
            P("section", None, "tensor"),
        ),
        check_vma=False,
    )
```

time: 1630 us -> 183 us (0.11)
  waiting for transfers between devices: 797 us -> 0 us
  blocking collectives: 524 us -> 0 us
  Pallas kernels: 0 us -> 174 us
  other arithmetic: 108 us -> 0 us
  local copies, waits for them, and re-layouts: 56.8 us -> 7.93 us
  matrix products: 47.7 us -> 0 us
  loops' own time: 38.8 us -> 0 us
  starting transfers between devices: 37.9 us -> 0 us
    psum x8 -> x0, blocking collectives: 524 us -> none  [the longest x7 461 us: backward_tick(): row_dot = lax.psum(jnp.sum(grad_h * x_own, axis=1, keepdims=True), 'tensor')]
    reduce_scatter x7 -> x0, waiting for transfers between devices: 498 us -> none  [backward_tick(): lax.psum_scatter(partial_value, 'tensor', scatter_dimension=1, tiled=True)]
    all_gather x7 -> x0, waiting for transfers between devices: 279 us -> none  [forward_tick(): whole = lax.all_gather(own, 'tensor', axis=1, tiled=True)]
    pallas_call x0 -> x1, Pallas kernels: none -> 174 us  [local(): pl.pallas_call(kernel, out_shape=(jax.ShapeDtypeStruct((1, 4, R, COLS), F...]
    dot_general x38 -> x0, matrix products: 47.7 us -> none  [the longest x23 30.1 us: contract(): lax.dot_general(left, right, (((left_dim,), (right_dim,)), ((), ())), pre...]
    another operation x16 -> x0, loops' own time: 38.8 us -> none  [the longest x1 12.5 us: local(): returned, accum = lax.fori_loop(0, ticks, backward_tick, (blank, accum))]
    ppermute x14 -> x0, starting transfers between devices: 37.8 us -> none  [passed_along(): return lax.ppermute(shard, axis, pairs)]
    dynamic_slice x42 -> x0, local copies, waits for them, and re-layouts: 31.3 us -> none  [pick(): return lax.dynamic_index_in_dim(array, index, 0, keepdims=False)]
  transfers between devices with their start and end apart: 28 -> 0, of which waited for: 21 -> 0; matrix products, arithmetic and copies ran while one was open for 6% -> 0% of each run, Pallas kernels for 0% -> 0%
where the time goes in v1:
time: 183 us
  Pallas kernels  174 us (95%)
  local copies, waits for them, and re-layouts  7.93 us (4%)
    pallas_call x1, Pallas kernels, local(): pl.pallas_call(kernel, out_shape=(jax.ShapeDtypeStruct((1, 4, R, COLS), F...  174 us
    unnamed x17, local copies, waits for them, and re-layouts  7.93 us

profile of v1, /device:TPU:0, one launch (start us, length us, event | category | flops | bytes accessed | tf_op | source)
XLA Modules:
  0.0 182.6 jit_solution(5436135060103728749)
XLA Ops:
  0.6 0.0 copy-start
  0.6 1.2 copy-done
  1.9 0.0 copy-start.1
  1.9 1.0 copy-done.1
  2.9 0.0 copy-start.2
  2.9 0.9 copy-done.2
  3.8 0.0 copy-start.3
  3.8 0.9 copy-done.3
  4.7 0.0 copy-start.4
  4.7 0.7 copy-done.4
  5.4 0.0 copy-start.5
  5.4 0.7 copy-done.5
  6.1 0.0 copy-start.6
  6.1 0.7 copy-done.6
  6.8 174.0 %shard_map.94 = (f32[1,4,16,128]{3,2,1,0:T(8,128)S(1)}, f32[1,4,16,128]{3,2,1,0:T(8,128)S(1)}, f32[1,4,128]{2,1,0:T(4,128)S(1)}) custom-call(s32[4]{0:T(128)S(1)} %copy-done.6, bf16[4,128,128]{2,1,0:T(8,128)(2,1)S(1)} %copy-done.2, bf16[4,128,128]{2,1,0:T(8,128)(2,1)S(1)} %copy-done.3, bf16[1,4096,128]{2,1,0:T(8,128)(2,1)S(1)} %copy-done, ...), custom_call_target="tpu_custom_call" | custom-call | tf_op jit(solution)/shard_map/pallas_call | solution.py:421
  180.8 0.6 copy.13
  181.4 0.6 copy.14
  182.0 0.6 copy.15
Async XLA Ops:
  0.6 1.2 copy-start
  1.9 1.0 copy-start.1
  2.9 0.9 copy-start.2
  3.8 0.9 copy-start.3
  4.7 0.7 copy-start.4
  5.4 0.7 copy-start.5
  6.1 0.7 copy-start.6

commit v2 on v1

v2 whole, which is shorter than its diff:
```python
import jax
import jax.numpy as jnp
from jax import lax
from jax.experimental import pallas as pl
from jax.experimental.pallas import tpu as pltpu
from jax.sharding import PartitionSpec as P

MESH = pl.DeviceIdType.MESH
F32 = jnp.float32
BF16 = jnp.bfloat16
HIGHEST = lax.Precision.HIGHEST

L = 4
TOK = 128
NH = 2
H = TOK // NH
D = 4096
R = 16
COLS = 128
CHIPS = 16
EXT = 16
RSB = H + EXT
HALF = D // 2
WCH = 8
WROWS = HALF // WCH


def hops(r):
    dz, dy = divmod(r, 4)
    return min(dz, 4 - dz) + min(dy, 4 - dy)


NEAR = sorted(range(CHIPS), key=hops)
GROUPS = [(1, 4), (5, 6), (11, 5)]
QUADS = [12, 8, 4, 0]


def inverse(p):
    dz, dy = divmod(NEAR[p], 4)
    return NEAR.index(((4 - dz) % 4) * 4 + (4 - dy) % 4)


def dot(a, b, ca, cb, precision=None):
    return lax.dot_general(
        a, b, (((ca,), (cb,)), ((), ())), precision=precision, preferred_element_type=F32
    )


def split3(v):
    hi = v.astype(BF16)
    rest = v - hi.astype(F32)
    mid = rest.astype(BF16)
    low = (rest - mid.astype(F32)).astype(BF16)
    return jnp.concatenate([hi, mid, low], axis=0)


def fold3(v):
    return v[0:R] + v[R : 2 * R] + v[2 * R : 3 * R]


def kernel(
    ten_ref, x_hbm, g_hbm, w_hbm, a_hbm, b_hbm, m_hbm,
    oa_ref, ob_ref, om_ref,
    w_buf, a_own, b_own, m_own, sm_src, mg_src, sm_buf, mg_buf, ag_a, xg, cur, grad,
    sv_branch, sv_low, sv_root, sv_norm, sv_scale,
    cs_src, cs_dst, ce_src, ce_dst, rs_src, rs_dst, own_sum, own_ext, lx_src, lx_dst, ex_src, ex_dst,
    res, od_src, od_dst,
    loc_sem, w_send, w_recv, sm_send, sm_recv, mg_send, mg_recv,
    aa_send, aa_recv, ac_send, ac_recv,
    ag_send, ag_recv, cf_send, cf_recv,
    cs_send, cs_recv, ce_send, ce_recv, rs_send, rs_recv,
    lx_send, lx_recv, ex_send, ex_recv, od_send, od_recv,
):
    s = lax.axis_index("section")
    t = lax.axis_index("tensor")
    z = t // 8
    y = (t // 2) % 4
    c = t % 2

    def plane(p):
        dz, dy = divmod(NEAR[p], 4)
        return (s, ((z + dz) % 4) * 8 + ((y + dy) % 4) * 2 + c)

    def source(p):
        dz, dy = divmod(NEAR[p], 4)
        return ((z + 4 - dz) % 4) * 4 + (y + 4 - dy) % 4

    partner = (s, t + 1 - 2 * c)

    def section(d):
        return ((s + d) % 4, t)

    def remote(src, dst, send, recv, device):
        return pltpu.make_async_remote_copy(
            src_ref=src, dst_ref=dst, send_sem=send, recv_sem=recv,
            device_id=device, device_id_type=MESH,
        )

    def every(n, fn):
        lax.fori_loop(0, n, lambda i, _: (fn(i), 0)[1], 0)

    def w_copy(layer, way, j, from_hbm=False):
        rows = pl.ds(way * HALF + j * WROWS, WROWS)
        src = w_hbm.at[0, rows] if from_hbm else w_buf.at[layer, rows]
        return remote(
            src, w_buf.at[layer, rows], w_send.at[layer, way, j], w_recv.at[layer, way, j],
            section(1 + 2 * way),
        )

    def sm_copy(d):
        return remote(sm_src.at[d], sm_buf.at[s], sm_send.at[d], sm_recv.at[d], section(d))

    def mg_copy(d):
        return remote(mg_src.at[d], mg_buf.at[s], mg_send.at[d], mg_recv.at[d], section(d))

    def aa_copy(p, g):
        return remote(ag_a.at[c, 0], ag_a.at[c, p], aa_send, aa_recv.at[g], plane(p))

    def aa_all(first, n, g):
        part = ag_a.at[c, pl.ds(first, n)]
        return remote(part, part, aa_send, aa_recv.at[g], partner)

    def ac_copy(core):
        return remote(ag_a.at[core], ag_a.at[core], ac_send, ac_recv, partner)

    def ag_copy(l, h, p, g):
        return remote(
            xg.at[l, h, c, 0], xg.at[l, h, c, p], ag_send.at[l, h], ag_recv.at[l, h, g], plane(p)
        )

    def ag_all(l, h, first, n, g):
        part = xg.at[l, h, c, pl.ds(first, n)]
        return remote(part, part, ag_send.at[l, h], ag_recv.at[l, h, g], partner)

    def cf_copy(l, h, first, n, g, core):
        part = xg.at[l, h, core, pl.ds(first, n)]
        return remote(part, part, cf_send.at[l, h, g], cf_recv.at[l, h, g], partner)

    def cs_copy(l, h, q):
        part = pl.ds(QUADS[q], 4)
        return remote(
            cs_src.at[l, h, part], cs_dst.at[l, h, part],
            cs_send.at[l, h, q], cs_recv.at[l, h, q], partner,
        )

    def ce_copy(l, h):
        return remote(
            ce_src.at[l, h], ce_dst.at[l, h], ce_send.at[l, h], ce_recv.at[l, h], partner
        )

    def rs_copy(l, h, p, g):
        return remote(
            rs_src.at[l, h, p], rs_dst.at[l, h, p], rs_send.at[l, h], rs_recv.at[l, h, g], plane(p)
        )

    def rs_all(l, h, first, n, g):
        part = pl.ds(first, n)
        return remote(
            rs_src.at[l, h, part], rs_dst.at[l, h, part],
            rs_send.at[l, h], rs_recv.at[l, h, g], partner,
        )

    def lx_copy():
        return remote(lx_src, lx_dst, lx_send, lx_recv, partner)

    def ex_copy(p):
        return remote(ex_src, ex_dst.at[p], ex_send, ex_recv, plane(p))

    def ex_all():
        part = ex_dst.at[pl.ds(1, CHIPS - 1)]
        return remote(part, part, ex_send, ex_recv, partner)

    def od_copy(d):
        return remote(
            od_src.at[(s + d) % 4], od_dst.at[s], od_send.at[d], od_recv.at[d], section(d)
        )

    def group_of(p):
        return [g for g, (first, n) in enumerate(GROUPS) if first <= p < first + n][0]

    own_x = pltpu.make_async_copy(x_hbm.at[s], cur, loc_sem.at[0])
    own_x.start()
    own_a = pltpu.make_async_copy(
        a_hbm.at[0, :, :, pl.ds(pl.multiple_of(t * COLS, COLS), COLS)], a_own, loc_sem.at[1]
    )
    own_a.start()
    own_b = pltpu.make_async_copy(b_hbm.at[0], b_own, loc_sem.at[2])
    own_b.start()
    own_m = pltpu.make_async_copy(m_hbm.at[0], m_own, loc_sem.at[3])
    own_m.start()
    own_w = pltpu.make_async_copy(w_hbm.at[0], w_buf.at[s], loc_sem.at[4])
    own_w.start()
    own_g = pltpu.make_async_copy(g_hbm.at[s], grad, loc_sem.at[5])
    own_g.start()

    def pick(values):
        out = jnp.int32(values[3])
        for i in range(3):
            out = jnp.where(s == i, jnp.int32(values[i]), out)
        return out

    def leave_own(way, cond):
        @pl.when(cond)
        def _():
            every(WCH, lambda j: w_copy(s, way, j, True).start())

    def pass_on(layer, way, j):
        w_copy(layer, way, j).wait_recv()
        w_copy(layer, way, j).start()

    leave_own(0, (s == 0) | (s == 3))
    leave_own(1, (s == 0) | (s == 1))

    own_x.wait()

    def send_block(l, h):
        xg[l, h, c, 0] = cur[h * H : (h + 1) * H]
        for p in reversed(range(1, CHIPS)):
            ag_copy(l, h, p, group_of(p)).start()
        cf_copy(l, h, 0, 1, 3, c).start()

    for h in range(NH):
        send_block(0, h)

    own_a.wait()
    own_b.wait()
    own_m.wait()
    for d in range(4):
        tenant = ten_ref[(s + d) % 4]
        pair = jnp.concatenate([a_own[tenant], b_own[tenant]], axis=0)
        mag = jnp.broadcast_to(m_own[pl.ds(tenant, 1), :], (8, COLS))
        if d == 0:
            sm_buf[s] = pair
            mg_buf[s] = mag
        else:
            sm_src[d] = pair
            mg_src[d] = mag
            sm_copy(d).start()
            mg_copy(d).start()
    for d in range(1, 4):
        sm_copy(d).wait_recv()
        mg_copy(d).wait_recv()
    for l in range(L):
        ag_a[c, 0, l * R : (l + 1) * R] = sm_buf[l, 0:R]
    for p in reversed(range(1, CHIPS)):
        aa_copy(p, group_of(p)).start()

    def round0(j):
        @pl.when((s == 1) | (s == 2))
        def _():
            pass_on(0, 0, j)

        @pl.when((s == 3) | (s == 2))
        def _():
            pass_on(0, 1, j)

    every(WCH, round0)
    own_w.wait()

    leave_own(0, s == 1)
    leave_own(1, s == 2)

    def round1_early(j):
        @pl.when(s == 0)
        def _():
            pass_on(3, 0, j)
            pass_on(1, 1, j)

    every(WCH, round1_early)

    for g, (first, n) in enumerate(GROUPS):
        aa_all(first, n, g).wait_recv()
    ac_copy(c).start()
    ac_copy(1 - c).wait_recv()

    def round1_late(j):
        @pl.when((s == 2) | (s == 3))
        def _():
            pass_on(1, 0, j)

        @pl.when((s == 1) | (s == 3))
        def _():
            pass_on(pick((0, 2, 0, 1)), 1, j)

    def round2_early(j):
        @pl.when(s == 1)
        def _():
            pass_on(3, 0, j)

        @pl.when(s == 0)
        def _():
            pass_on(2, 1, j)

    def round2_late(j):
        @pl.when((s == 3) | (s == 0))
        def _():
            pass_on(2, 0, j)

        @pl.when((s == 2) | (s == 1))
        def _():
            pass_on(3, 1, j)

    def a_rows(l, p):
        rows = pl.ds(pl.multiple_of(l * R, R), R)
        return jnp.concatenate([ag_a[0, p, rows, :], ag_a[1, p, rows, :]], axis=1)

    def w_rows(l, p):
        return w_buf[l, pl.ds(pl.multiple_of(source(p) * 256, 256), 256), :]

    def column_norms(l):
        def squares(i, total):
            rows = w_buf[l, pl.ds(pl.multiple_of(i * 256, 256), 256), :].astype(F32)
            return total + jnp.sum((rows * rows).reshape(32, 8, COLS), axis=0)

        base_sq = jnp.sum(
            lax.fori_loop(0, 16, squares, jnp.zeros((8, COLS), F32)), axis=0, keepdims=True
        )
        cross = jnp.zeros((R, COLS), F32)
        gram = jnp.zeros((R, R), F32)
        for p in range(CHIPS):
            a_p = a_rows(l, p)
            cross = cross + dot(a_p, w_rows(l, p), 1, 0)
            gram = gram + dot(a_p, a_p, 1, 1)
        b_wide = sm_buf[l, R : 2 * R].astype(F32)
        quad = dot(gram, b_wide, 1, 0, HIGHEST)
        total = base_sq + jnp.sum(b_wide * (2.0 * cross + quad), axis=0, keepdims=True)
        norm = jnp.sqrt(total + 1e-06)
        sv_norm[l] = jnp.broadcast_to(norm, (8, COLS))
        sv_scale[l] = jnp.broadcast_to(mg_buf[l, 0:1] / norm, (8, COLS))

    def forward(l, _):
        @pl.when(l == 1)
        def _():
            every(WCH, round1_late)
            leave_own(0, s == 2)
            leave_own(1, s == 3)
            every(WCH, round2_early)

        @pl.when(l == 2)
        def _():
            every(WCH, round2_late)

        @pl.when((s + 1) % 4 == l)
        def _():
            every(WCH, lambda j: w_copy(l, 0, j).wait_recv())

        @pl.when((s + 3) % 4 == l)
        def _():
            every(WCH, lambda j: w_copy(l, 1, j).wait_recv())

        column_norms(l)
        for h in range(NH):
            tokens = slice(h * H, (h + 1) * H)
            acc = jnp.zeros((H, COLS), F32)
            low_acc = jnp.zeros((H, R), F32)
            ssq = jnp.zeros((H, COLS), F32)

            def use(first, n, g, acc, low_acc, ssq):
                cf_copy(l, h, first, n, g, 1 - c).wait_recv()
                for p in range(first, first + n):
                    both = jnp.concatenate([xg[l, h, 0, p], xg[l, h, 1, p]], axis=1)
                    acc = acc + dot(both, w_rows(l, p), 1, 0)
                    low_acc = low_acc + dot(both, a_rows(l, p), 1, 1)
                    wide = both.astype(F32)
                    wide = wide * wide
                    ssq = ssq + wide[:, 0:COLS] + wide[:, COLS:]
                return acc, low_acc, ssq

            before = (0, 1, 3)
            for g, (first, n) in enumerate(GROUPS):
                ag_all(l, h, first, n, g).wait_recv()
                cf_copy(l, h, first, n, g, c).start()
                acc, low_acc, ssq = use(*before, acc, low_acc, ssq)
                before = (first, n, g)
            acc, low_acc, ssq = use(*before, acc, low_acc, ssq)

            mean = jnp.sum(ssq, axis=1, keepdims=True) * (1.0 / D)
            root = jnp.sqrt(mean + 1e-05)
            inv = 1.0 / root
            low = (low_acc * inv).astype(BF16)
            branch = acc * inv + dot(low, sm_buf[l, R : 2 * R], 1, 0)
            sv_branch[l, tokens] = branch
            sv_low[l, tokens] = low
            sv_root[l, tokens] = jnp.broadcast_to(root, (H, COLS))
            state = cur[tokens].astype(F32) + sv_scale[l, 0:1] * branch
            cur[tokens] = state.astype(BF16)

            @pl.when(l < L - 1)
            def _():
                send_block(l + 1, h)

        return 0

    lax.fori_loop(0, L, forward, 0)

    own_g.wait()

    def local_grads(l, h0, h1, first):
        tokens = slice(h0, h1)
        up = grad[tokens].astype(F32)
        branch = sv_branch[l, tokens]
        grad_branch = (up * sv_scale[l, 0:1]).astype(BF16)
        gm = jnp.sum(up * branch, axis=0, keepdims=True) / sv_norm[l, 0:1]
        gm = jnp.broadcast_to(gm, (8, COLS))
        gb = dot(sv_low[l, tokens], grad_branch, 0, 0)
        if not first:
            gb = gb + res[l, R : 2 * R]
            gm = gm + res[l, 2 * R : 2 * R + 8]
        res[l, R : 2 * R] = gb
        res[l, 2 * R : 2 * R + 8] = gm
        rank_t = dot(sm_buf[l, R : 2 * R], grad_branch, 1, 1)
        return branch, grad_branch, rank_t

    def begin(l, h):
        tokens = slice(h * H, (h + 1) * H)
        branch, grad_branch, rank_t = local_grads(l, h * H, (h + 1) * H, h == 0)
        prod = grad_branch.astype(F32) * branch * sv_root[l, tokens]
        row = jnp.sum(prod.T, axis=0, keepdims=True)
        row = jnp.concatenate([row, jnp.zeros((1, COLS - H), F32)], axis=1)
        ce_src[l, h] = jnp.concatenate(
            [
                jnp.concatenate([rank_t[0:8], rank_t[8:16]], axis=1),
                jnp.broadcast_to(row, (8, COLS)),
            ],
            axis=0,
        )
        ce_copy(l, h).start()
        rank = rank_t.T
        rank_hi = rank.astype(BF16)
        rank_lo = (rank - rank_hi.astype(F32)).astype(BF16)
        rank_two = jnp.concatenate([rank_hi, rank_lo], axis=1)

        def part(p, core):
            q = inverse(p)
            start = pl.multiple_of(source(q) * 256 + core * COLS, COLS)
            rows = w_buf[l, pl.ds(start, COLS), :]
            a_q = ag_a[core, q, pl.ds(pl.multiple_of(l * R, R), R), :]
            return dot(grad_branch, rows, 1, 1) + dot(
                rank_two, jnp.concatenate([a_q, a_q], axis=0), 1, 0
            )

        def away(q):
            for p in range(QUADS[q], QUADS[q] + 4):
                cs_src[l, h, p] = part(p, 1 - c).astype(BF16)
            cs_copy(l, h, q).start()

        away(0)
        away(1)
        ext_b = None
        for q in range(4):
            if q < 2:
                away(q + 2)
            mine = {p: part(p, c) for p in range(QUADS[q], QUADS[q] + 4)}
            if q == 0:
                ce_copy(l, h).wait_recv()
                ext = ce_src[l, h] + ce_dst[l, h]
                row = ext[8:16, 0:H]
                row_hi = row.astype(BF16).astype(F32)
                ext = jnp.concatenate(
                    [ext[0:8], jnp.concatenate([row_hi, row - row_hi], axis=1)], axis=0
                )
                own_ext[h] = ext
                ext_b = ext.astype(BF16)
            cs_copy(l, h, q).wait_recv()
            for p in reversed(range(QUADS[q], QUADS[q] + 4)):
                total = mine[p] + cs_dst[l, h, p].astype(F32)
                if p:
                    rs_src[l, h, p, 0:H] = total.astype(BF16)
                    rs_src[l, h, p, H:RSB] = ext_b
                    rs_copy(l, h, p, group_of(p)).start()
                else:
                    own_sum[h] = total

    def adapter_grad(l, h0, h1, rank_sum, first):
        tokens = slice(h0, h1)
        if h1 - h0 == TOK:
            x_own = jnp.concatenate([xg[l, i, c, 0] for i in range(NH)], axis=0)
        else:
            x_own = xg[l, h0 // H, c, 0]
        normed = (x_own.astype(F32) / sv_root[l, tokens]).astype(BF16)
        ga = fold3(dot(split3(rank_sum), normed, 1, 0))
        if not first:
            ga = ga + res[l, 0:R]
        res[l, 0:R] = ga

    def finish(l, h):
        tokens = slice(h * H, (h + 1) * H)
        total = jnp.concatenate([own_sum[h], own_ext[h]], axis=0)
        for g, (first, n) in enumerate(GROUPS):
            rs_all(l, h, first, n, g).wait_recv()
            for p in range(first, first + n):
                total = total + rs_dst[l, h, p].astype(F32)
        grad_h = total[0:H]
        rank = total[H : H + 8]
        rank_sum = jnp.concatenate([rank[:, 0:H], rank[:, H:]], axis=0)
        row = total[H + 8 : H + 9]
        row = row[:, 0:H] + row[:, H:]
        row_dot = jnp.broadcast_to(row, (COLS, H)).T
        up = grad[tokens].astype(F32)
        x_own = xg[l, h, c, 0].astype(F32)
        inv = 1.0 / sv_root[l, tokens]
        state = up + (grad_h - x_own * (row_dot * (inv * inv) * (1.0 / D))) * inv
        grad[tokens] = state.astype(BF16)
        return rank_sum

    for h in range(NH):
        begin(L - 1, h)

    def backward(i, _):
        l = L - 1 - i
        for h in range(NH):
            rank_sum = finish(l, h)

            @pl.when(l > 1)
            def _():
                begin(l - 1, h)

            adapter_grad(l, h * H, (h + 1) * H, rank_sum, h == 0)
        return 0

    lax.fori_loop(0, L - 1, backward, 0)

    _, _, rank_t = local_grads(0, 0, TOK, True)
    sum_a = jnp.zeros((1, COLS), F32)
    sum_b = jnp.zeros((1, COLS), F32)
    sum_m = jnp.zeros((1, COLS), F32)
    for l in range(L):
        if l:
            ga = res[l, 0:R]
            sum_a = sum_a + jnp.sum(ga * ga, axis=0, keepdims=True)
        gb = res[l, R : 2 * R]
        sum_b = sum_b + jnp.sum(gb * gb, axis=0, keepdims=True)
        gm = res[l, 2 * R : 2 * R + 1]
        sum_m = sum_m + gm * gm
    lx_src[...] = jnp.concatenate(
        [rank_t, sum_a, sum_b, sum_m, jnp.zeros((5, COLS), F32)], axis=0
    )
    lx_copy().start()
    lx_copy().wait_recv()
    ext = lx_src[...] + lx_dst[...]
    ex_src[...] = ext
    for p in reversed(range(1, CHIPS)):
        ex_copy(p).start()
    outer = jnp.zeros((TOK, TOK), F32)
    for p in range(CHIPS):
        both = jnp.concatenate(
            [
                jnp.concatenate([xg[0, h, 0, p], xg[0, h, 1, p]], axis=1)
                for h in range(NH)
            ],
            axis=0,
        )
        outer = outer + dot(both, both, 1, 1)
    inv = 1.0 / sv_root[0]
    outer = outer * inv * inv.T
    ex_all().wait_recv()
    for p in range(1, CHIPS):
        ext = ext + ex_dst[p]
    rank_sum = ext[0:R]
    adapter_grad(0, 0, TOK, rank_sum, True)
    sq = rank_sum * dot(rank_sum, outer, 1, 0, HIGHEST)

    def norm_of(v, count):
        return 1.0 / jnp.sqrt(jnp.sum(v, axis=1, keepdims=True) * (1.0 / count) + 1e-06)

    by_a = norm_of(ext[R : R + 1] + jnp.sum(sq, axis=0, keepdims=True), L * R * D)
    by_b = norm_of(ext[R + 1 : R + 2], L * R * D)
    by_m = norm_of(ext[R + 2 : R + 3], L * D)
    for l in range(L):
        od_src[l, 0:R] = res[l, 0:R] * by_a
        od_src[l, R : 2 * R] = res[l, R : 2 * R] * by_b
        od_src[l, 2 * R : 2 * R + 8] = res[l, 2 * R : 2 * R + 8] * by_m
    for d in (2, 1, 3):
        od_copy(d).start()
    od_dst[s] = od_src[s]

    def drain_w(j):
        for h in range(3):
            w_copy((s + 4 - h) % 4, 0, j).wait_send()
            w_copy((s + h) % 4, 1, j).wait_send()

    every(WCH, drain_w)
    aa_all(1, CHIPS - 1, 0).wait_send()
    ac_copy(c).wait_send()

    def drain_l(l):
        for h in range(NH):
            ag_all(l, h, 1, CHIPS - 1, 0).wait_send()
            cf_copy(l, h, 0, 1, 3, c).wait_send()
            for g, (first, n) in enumerate(GROUPS):
                cf_copy(l, h, first, n, g, c).wait_send()

    every(L, drain_l)

    def drain_b(i):
        l = i + 1
        for h in range(NH):
            rs_all(l, h, 1, CHIPS - 1, 0).wait_send()
            ce_copy(l, h).wait_send()
            for q in range(4):
                cs_copy(l, h, q).wait_send()

    every(L - 1, drain_b)
    lx_copy().wait_send()
    ex_all().wait_send()
    for d in range(1, 4):
        sm_copy(d).wait_send()
        mg_copy(d).wait_send()

    for d in (1, 3, 2):
        od_copy(d).wait_recv()
    for tenant in range(4):
        out = jnp.zeros((2 * R + 8, COLS), F32)
        for k in range(4):
            out = jnp.where(ten_ref[k] == tenant, od_dst[k], out)
        oa_ref[0, tenant] = out[0:R]
        ob_ref[0, tenant] = out[R : 2 * R]
        om_ref[0, pl.ds(tenant, 1), :] = out[2 * R : 2 * R + 1]
    for d in range(1, 4):
        od_copy(d).wait_send()


def local(inputs, grad_out, tenants, base_weight, adapter_a, adapter_b, magnitude):
    vmem = pl.BlockSpec(memory_space=pltpu.VMEM)
    hbm = pl.BlockSpec(memory_space=pl.ANY)
    dma = pltpu.SemaphoreType.DMA
    return pl.pallas_call(
        kernel,
        out_shape=(
            jax.ShapeDtypeStruct((1, 4, R, COLS), F32),
            jax.ShapeDtypeStruct((1, 4, R, COLS), F32),
            jax.ShapeDtypeStruct((1, 4, COLS), F32),
        ),
        in_specs=[pl.BlockSpec(memory_space=pltpu.SMEM)] + [hbm] * 6,
        out_specs=(vmem, vmem, vmem),
        scratch_shapes=[
            pltpu.VMEM((L, D, COLS), BF16),
            pltpu.VMEM((4, R, COLS), BF16),
            pltpu.VMEM((4, R, COLS), BF16),
            pltpu.VMEM((4, COLS), F32),
            pltpu.VMEM((4, 2 * R, COLS), BF16),
            pltpu.VMEM((4, 8, COLS), F32),
            pltpu.VMEM((4, 2 * R, COLS), BF16),
            pltpu.VMEM((4, 8, COLS), F32),
            pltpu.VMEM((2, CHIPS, L * R, COLS), BF16),
            pltpu.VMEM((L, NH, 2, CHIPS, H, COLS), BF16),
            pltpu.VMEM((TOK, COLS), BF16),
            pltpu.VMEM((TOK, COLS), BF16),
            pltpu.VMEM((L, TOK, COLS), F32),
            pltpu.VMEM((L, TOK, R), BF16),
            pltpu.VMEM((L, TOK, COLS), F32),
            pltpu.VMEM((L, 8, COLS), F32),
            pltpu.VMEM((L, 8, COLS), F32),
            pltpu.VMEM((L, NH, CHIPS, H, COLS), BF16),
            pltpu.VMEM((L, NH, CHIPS, H, COLS), BF16),
            pltpu.VMEM((L, NH, EXT, COLS), F32),
            pltpu.VMEM((L, NH, EXT, COLS), F32),
            pltpu.VMEM((L, NH, CHIPS, RSB, COLS), BF16),
            pltpu.VMEM((L, NH, CHIPS, RSB, COLS), BF16),
            pltpu.VMEM((NH, H, COLS), F32),
            pltpu.VMEM((NH, EXT, COLS), F32),
            pltpu.VMEM((R + 8, TOK), F32),
            pltpu.VMEM((R + 8, TOK), F32),
            pltpu.VMEM((R + 8, TOK), F32),
            pltpu.VMEM((CHIPS, R + 8, TOK), F32),
            pltpu.VMEM((L, 2 * R + 8, COLS), F32),
            pltpu.VMEM((L, 2 * R + 8, COLS), F32),
            pltpu.VMEM((L, 2 * R + 8, COLS), F32),
            dma((6,)),
            dma((L, 2, WCH)),
            dma((L, 2, WCH)),
            dma((4,)),
            dma((4,)),
            dma((4,)),
            dma((4,)),
            dma,
            dma((3,)),
            dma,
            dma,
            dma((L, NH)),
            dma((L, NH, 3)),
            dma((L, NH, 4)),
            dma((L, NH, 4)),
            dma((L, NH, 4)),
            dma((L, NH, 4)),
            dma((L, NH)),
            dma((L, NH)),
            dma((L, NH)),
            dma((L, NH, 3)),
            dma,
            dma,
            dma,
            dma,
            dma((4,)),
            dma((4,)),
        ],
        compiler_params=pltpu.CompilerParams(
            has_side_effects=True, vmem_limit_bytes=60 * 2**20
        ),
    )(tenants, inputs, grad_out, base_weight, adapter_a, adapter_b, magnitude)


def solution(mesh):
    return jax.shard_map(
        local,
        mesh=mesh,
        in_specs=(
            P(None, None, "tensor"),
            P(None, None, "tensor"),
            P(),
            P("section", None, "tensor"),
            P("section", None, None, None),
            P("section", None, None, "tensor"),
            P("section", None, "tensor"),
        ),
        out_specs=(
            P("section", None, None, "tensor"),
            P("section", None, None, "tensor"),
            P("section", None, "tensor"),
        ),
        check_vma=False,
    )
```

time: 183 us -> 149 us (0.81)
  Pallas kernels: 174 us -> 146 us
  local copies, waits for them, and re-layouts: 7.93 us -> 2.64 us
    pallas_call x1, Pallas kernels: 174 us -> 146 us  [local(): pl.pallas_call(kernel, out_shape=(jax.ShapeDtypeStruct((1, 4, R, COLS), F...]
    unnamed x17 -> x7, local copies, waits for them, and re-layouts: 7.93 us -> 2.64 us
where the time goes in v2:
time: 149 us
  Pallas kernels  146 us (98%)
  local copies, waits for them, and re-layouts  2.64 us (2%)
    pallas_call x1, Pallas kernels, local(): pl.pallas_call(kernel, out_shape=(jax.ShapeDtypeStruct((1, 4, R, COLS), F...  146 us

profile of v2, /device:TPU:0, one launch (start us, length us, event | category | flops | bytes accessed | tf_op | source)
XLA Modules:
  0.0 149.1 jit_solution(6304026742715111098)
XLA Ops:
  0.6 145.9 %shard_map.94 = (f32[1,4,16,128]{3,2,1,0:T(8,128)}, f32[1,4,16,128]{3,2,1,0:T(8,128)}, f32[1,4,128]{2,1,0:T(4,128)}) custom-call(s32[4]{0:T(128)} %ten_ref.1, bf16[4,128,128]{2,1,0:T(8,128)(2,1)} %x_hbm.1, bf16[4,128,128]{2,1,0:T(8,128)(2,1)} %g_hbm.1, bf16[1,4096,128]{2,1,0:T(8,128)(2,1)} %w_hbm.1, bf16[1,4,16,4096]{3,2,1,0:T(8,128)(2,1)} %a_hbm.1, ...), custom_call_target="tpu_custom_call" | custom-call | tf_op jit(solution)/shard_map/pallas_call | solution.py:627
  146.5 0.0 copy-start
  146.5 1.4 copy.13
  147.9 0.0 copy-done
  147.9 0.0 copy-start.1
  147.9 0.6 copy.14
  148.5 0.1 copy-done.1
  148.6 0.6 copy.15
Async XLA Ops:
  146.5 1.4 copy-start
  147.9 0.7 copy-start.1

commit v3 on v2

--- a/solution.py
+++ b/solution.py
@@ -99,12 +99,25 @@
     def every(n, fn):
         lax.fori_loop(0, n, lambda i, _: (fn(i), 0)[1], 0)
 
-    def w_copy(layer, way, j, from_hbm=False):
-        rows = pl.ds(way * HALF + j * WROWS, WROWS)
-        src = w_hbm.at[0, rows] if from_hbm else w_buf.at[layer, rows]
-        return remote(
-            src, w_buf.at[layer, rows], w_send.at[layer, way, j], w_recv.at[layer, way, j],
+    def w_own(way, half, j):
+        rows = pl.ds(half * HALF + j * WROWS, WROWS)
+        return remote(
+            w_hbm.at[0, rows], w_buf.at[s, rows], w_send.at[0, way], w_recv.at[s, half, j],
             section(1 + 2 * way),
+        )
+
+    def w_pass(layer, half, j):
+        rows = pl.ds(half * HALF + j * WROWS, WROWS)
+        return remote(
+            w_buf.at[layer, rows], w_buf.at[layer, rows], w_send.at[1, half],
+            w_recv.at[layer, half, j], section(1 + 2 * half),
+        )
+
+    def w_left(kind, way, n):
+        rows = pl.ds(0, n)
+        return remote(
+            w_hbm.at[0, rows], w_buf.at[s, rows], w_send.at[kind, way], w_recv.at[0, 0, 0],
+            section(1),
         )
 
     def sm_copy(d):
@@ -193,35 +206,10 @@
     own_g = pltpu.make_async_copy(g_hbm.at[s], grad, loc_sem.at[5])
     own_g.start()
 
-    def pick(values):
-        out = jnp.int32(values[3])
-        for i in range(3):
-            out = jnp.where(s == i, jnp.int32(values[i]), out)
-        return out
-
-    def leave_own(way, cond):
-        @pl.when(cond)
-        def _():
-            every(WCH, lambda j: w_copy(s, way, j, True).start())
-
-    def pass_on(layer, way, j):
-        w_copy(layer, way, j).wait_recv()
-        w_copy(layer, way, j).start()
-
-    leave_own(0, (s == 0) | (s == 3))
-    leave_own(1, (s == 0) | (s == 1))
-
-    own_x.wait()
-
-    def send_block(l, h):
-        xg[l, h, c, 0] = cur[h * H : (h + 1) * H]
-        for p in reversed(range(1, CHIPS)):
-            ag_copy(l, h, p, group_of(p)).start()
-        cf_copy(l, h, 0, 1, 3, c).start()
-
-    for h in range(NH):
-        send_block(0, h)
-
+    barrier = pltpu.get_barrier_semaphore()
+    peers = [plane(p) for p in range(1, CHIPS)] + [section(d) for d in (1, 2, 3)] + [partner]
+    for peer in peers:
+        pl.semaphore_signal(barrier, inc=1, device_id=peer, device_id_type=MESH)
     own_a.wait()
     own_b.wait()
     own_m.wait()
@@ -235,8 +223,41 @@
         else:
             sm_src[d] = pair
             mg_src[d] = mag
-            sm_copy(d).start()
-            mg_copy(d).start()
+    own_x.wait()
+
+    pl.semaphore_wait(barrier, len(peers))
+
+    for d in (2, 1, 3):
+        sm_copy(d).start()
+        mg_copy(d).start()
+
+    def send_block(l, h):
+        xg[l, h, c, 0] = cur[h * H : (h + 1) * H]
+        for p in reversed(range(1, CHIPS)):
+            ag_copy(l, h, p, group_of(p)).start()
+        cf_copy(l, h, 0, 1, 3, c).start()
+
+    def send_own(way):
+        for half in (way, 1 - way):
+            every(WCH, lambda j: w_own(way, half, j).start())
+
+    def pass_on(layer, half):
+        def one(j):
+            w_pass(layer, half, j).wait_recv()
+            w_pass(layer, half, j).start()
+
+        every(WCH, one)
+
+    @pl.when(s != 1)
+    def _():
+        send_own(0)
+
+    @pl.when(s != 3)
+    def _():
+        send_own(1)
+
+    for h in range(NH):
+        send_block(0, h)
     for d in range(1, 4):
         sm_copy(d).wait_recv()
         mg_copy(d).wait_recv()
@@ -245,60 +266,34 @@
     for p in reversed(range(1, CHIPS)):
         aa_copy(p, group_of(p)).start()
 
-    def round0(j):
-        @pl.when((s == 1) | (s == 2))
-        def _():
-            pass_on(0, 0, j)
-
-        @pl.when((s == 3) | (s == 2))
-        def _():
-            pass_on(0, 1, j)
-
-    every(WCH, round0)
+    @pl.when(s == 1)
+    def _():
+        pass_on(0, 0)
+        send_own(0)
+        w_left(0, 1, D).wait_send()
+        pass_on(2, 1)
+
+    @pl.when(s == 3)
+    def _():
+        pass_on(0, 1)
+        send_own(1)
+        w_left(0, 0, D).wait_send()
+        pass_on(2, 0)
+
     own_w.wait()
-
-    leave_own(0, s == 1)
-    leave_own(1, s == 2)
-
-    def round1_early(j):
-        @pl.when(s == 0)
-        def _():
-            pass_on(3, 0, j)
-            pass_on(1, 1, j)
-
-    every(WCH, round1_early)
 
     for g, (first, n) in enumerate(GROUPS):
         aa_all(first, n, g).wait_recv()
     ac_copy(c).start()
     ac_copy(1 - c).wait_recv()
 
-    def round1_late(j):
-        @pl.when((s == 2) | (s == 3))
+    def pass_late():
+        @pl.when((s == 0) | (s == 2))
         def _():
-            pass_on(1, 0, j)
-
-        @pl.when((s == 1) | (s == 3))
-        def _():
-            pass_on(pick((0, 2, 0, 1)), 1, j)
-
-    def round2_early(j):
-        @pl.when(s == 1)
-        def _():
-            pass_on(3, 0, j)
-
-        @pl.when(s == 0)
-        def _():
-            pass_on(2, 1, j)
-
-    def round2_late(j):
-        @pl.when((s == 3) | (s == 0))
-        def _():
-            pass_on(2, 0, j)
-
-        @pl.when((s == 2) | (s == 1))
-        def _():
-            pass_on(3, 1, j)
+            w_left(0, 0, D).wait_send()
+            w_left(0, 1, D).wait_send()
+            pass_on((s + 3) % 4, 0)
+            pass_on((s + 1) % 4, 1)
 
     def a_rows(l, p):
         rows = pl.ds(pl.multiple_of(l * R, R), R)
@@ -331,22 +326,17 @@
     def forward(l, _):
         @pl.when(l == 1)
         def _():
-            every(WCH, round1_late)
-            leave_own(0, s == 2)
-            leave_own(1, s == 3)
-            every(WCH, round2_early)
-
-        @pl.when(l == 2)
+            pass_late()
+
+        behind = (s + 4 - l) % 4
+
+        @pl.when(behind >= 2)
         def _():
-            every(WCH, round2_late)
-
-        @pl.when((s + 1) % 4 == l)
+            every(WCH, lambda j: w_pass(l, 0, j).wait_recv())
+
+        @pl.when((behind == 1) | (behind == 2))
         def _():
-            every(WCH, lambda j: w_copy(l, 0, j).wait_recv())
-
-        @pl.when((s + 3) % 4 == l)
-        def _():
-            every(WCH, lambda j: w_copy(l, 1, j).wait_recv())
+            every(WCH, lambda j: w_pass(l, 1, j).wait_recv())
 
         column_norms(l)
         for h in range(NH):
@@ -574,12 +564,16 @@
         od_copy(d).start()
     od_dst[s] = od_src[s]
 
-    def drain_w(j):
-        for h in range(3):
-            w_copy((s + 4 - h) % 4, 0, j).wait_send()
-            w_copy((s + h) % 4, 1, j).wait_send()
-
-    every(WCH, drain_w)
+    @pl.when(s == 1)
+    def _():
+        w_left(0, 0, D).wait_send()
+
+    @pl.when(s == 3)
+    def _():
+        w_left(0, 1, D).wait_send()
+
+    w_left(1, 0, HALF).wait_send()
+    w_left(1, 1, HALF).wait_send()
     aa_all(1, CHIPS - 1, 0).wait_send()
     ac_copy(c).wait_send()
 
@@ -667,7 +661,7 @@
             pltpu.VMEM((L, 2 * R + 8, COLS), F32),
             pltpu.VMEM((L, 2 * R + 8, COLS), F32),
             dma((6,)),
-            dma((L, 2, WCH)),
+            dma((2, 2)),
             dma((L, 2, WCH)),
             dma((4,)),
             dma((4,)),
@@ -695,7 +689,7 @@
             dma((4,)),
         ],
         compiler_params=pltpu.CompilerParams(
-            has_side_effects=True, vmem_limit_bytes=60 * 2**20
+            collective_id=0, has_side_effects=True, vmem_limit_bytes=60 * 2**20
         ),
     )(tenants, inputs, grad_out, base_weight, adapter_a, adapter_b, magnitude)
 

time: 149 us -> 118 us (0.79)
  Pallas kernels: 146 us -> 114 us
    pallas_call x1, Pallas kernels: 146 us -> 114 us  [local(): pl.pallas_call(kernel, out_shape=(jax.ShapeDtypeStruct((1, 4, R, COLS), F...]
where the time goes in v3:
time: 118 us
  Pallas kernels  114 us (97%)
  local copies, waits for them, and re-layouts  2.64 us (2%)
    pallas_call x1, Pallas kernels, local(): pl.pallas_call(kernel, out_shape=(jax.ShapeDtypeStruct((1, 4, R, COLS), F...  114 us
    unnamed x7, local copies, waits for them, and re-layouts  2.64 us

profile of v3, /device:TPU:0, one launch (start us, length us, event | category | flops | bytes accessed | tf_op | source)
XLA Modules:
  0.0 117.8 jit_solution(5563974233952051445)
XLA Ops:
  0.6 114.5 %shard_map.94 = (f32[1,4,16,128]{3,2,1,0:T(8,128)}, f32[1,4,16,128]{3,2,1,0:T(8,128)}, f32[1,4,128]{2,1,0:T(4,128)}) custom-call(s32[4]{0:T(128)} %ten_ref.1, bf16[4,128,128]{2,1,0:T(8,128)(2,1)} %x_hbm.1, bf16[4,128,128]{2,1,0:T(8,128)(2,1)} %g_hbm.1, bf16[1,4096,128]{2,1,0:T(8,128)(2,1)} %w_hbm.1, bf16[1,4,16,4096]{3,2,1,0:T(8,128)(2,1)} %a_hbm.1, ...), custom_call_target="tpu_custom_call" | custom-call | tf_op jit(solution)/shard_map/pallas_call | solution.py:621
  115.1 0.0 copy-start
  115.1 1.4 %copy.13 = f32[1,4,16,128]{3,2,1,0:T(8,128)} copy(f32[1,4,16,128]{3,2,1,0:T(8,128)} %get-tuple-element.6) | data formatting | bytes 65536
  116.5 0.0 copy-done
  116.5 0.0 copy-start.1
  116.5 0.6 copy.14
  117.1 0.1 copy-done.1
  117.2 0.6 copy.15
Async XLA Ops:
  115.1 1.4 %copy-start = (f32[1,4,16,128]{3,2,1,0:T(8,128)S(1)}, f32[1,4,16,128]{3,2,1,0:T(8,128)}, u32[]{:S(2)}) copy-start(f32[1,4,16,128]{3,2,1,0:T(8,128)} %get-tuple-element.7) | copy-start | bytes 98308
  116.5 0.7 copy-start.1

commit v4 on v3

--- a/solution.py
+++ b/solution.py
@@ -18,11 +18,55 @@
 R = 16
 COLS = 128
 CHIPS = 16
-EXT = 16
-RSB = H + EXT
-HALF = D // 2
-WCH = 8
-WROWS = HALF // WCH
+RSB = [H] * (NH - 1) + [H + R]
+WCH = 16
+WROWS = D // WCH
+
+ROUTES = {
+    0: {
+        0: [(0, 0, 0, 12), (1, 0, 12, 4), (1, 0, 8, 4), (1, 0, 4, 4), (1, 1, 12, 4), (1, 1, 8, 4)],
+        1: [(1, 1, 6, 2), (0, 3, 0, 16)],
+        2: [(1, 2, 12, 4)],
+    },
+    1: {
+        0: [
+            (1, 1, 12, 4), (1, 1, 8, 4), (1, 1, 6, 2), (1, 1, 0, 6),
+            (0, 0, 0, 8), (0, 1, 0, 12), (1, 2, 12, 4), (1, 2, 8, 4),
+        ],
+        2: [(0, 3, 0, 8)],
+    },
+    2: {
+        0: [
+            (0, 2, 0, 8), (1, 2, 12, 4), (1, 2, 8, 4),
+            (0, 0, 0, 4), (1, 0, 12, 4), (0, 1, 0, 6), (1, 2, 0, 8),
+        ],
+        1: [(0, 2, 8, 4)],
+    },
+    3: {
+        0: [(0, 3, 0, 16), (1, 0, 12, 4), (1, 0, 8, 4), (0, 2, 0, 8), (1, 1, 12, 4)],
+        1: [(1, 3, 8, 8)],
+    },
+}
+
+
+def sent(section, way):
+    return sum(e[3] for stage in ROUTES[section].values() for e in stage if e[0] == way)
+
+
+def awaited(section, layer, stage):
+    done = set()
+    for k in range(stage + 1):
+        for event in ROUTES[section].get(k, []):
+            if event[1] == layer:
+                done |= set(range(event[2], event[2] + event[3]))
+    left = [j for j in range(WCH) if j not in done]
+    runs = []
+    for j in left:
+        if runs and runs[-1][0] + runs[-1][1] == j:
+            runs[-1][1] += 1
+        else:
+            runs.append([j, 1])
+    return runs
 
 
 def hops(r):
@@ -62,8 +106,8 @@
     ten_ref, x_hbm, g_hbm, w_hbm, a_hbm, b_hbm, m_hbm,
     oa_ref, ob_ref, om_ref,
     w_buf, a_own, b_own, m_own, sm_src, mg_src, sm_buf, mg_buf, ag_a, xg, cur, grad,
-    sv_branch, sv_low, sv_root, sv_norm, sv_scale,
-    cs_src, cs_dst, ce_src, ce_dst, rs_src, rs_dst, own_sum, own_ext, lx_src, lx_dst, ex_src, ex_dst,
+    sv_branch, sv_low, sv_root, sv_norm, sv_scale, sv_gb,
+    mine_buf, cs_src, cs_dst, ce_src, ce_dst, rs_src, rs_dst, own_sum, own_ext, rank_buf, lx_src, lx_dst, ex_src, ex_dst,
     res, od_src, od_dst,
     loc_sem, w_send, w_recv, sm_send, sm_recv, mg_send, mg_recv,
     aa_send, aa_recv, ac_send, ac_recv,
@@ -99,26 +143,21 @@
     def every(n, fn):
         lax.fori_loop(0, n, lambda i, _: (fn(i), 0)[1], 0)
 
-    def w_own(way, half, j):
-        rows = pl.ds(half * HALF + j * WROWS, WROWS)
+    def w_copy(way, layer, j, own):
+        rows = pl.ds(j * WROWS, WROWS)
+        src = w_hbm.at[0, rows] if own else w_buf.at[layer, rows]
         return remote(
-            w_hbm.at[0, rows], w_buf.at[s, rows], w_send.at[0, way], w_recv.at[s, half, j],
-            section(1 + 2 * way),
-        )
-
-    def w_pass(layer, half, j):
-        rows = pl.ds(half * HALF + j * WROWS, WROWS)
-        return remote(
-            w_buf.at[layer, rows], w_buf.at[layer, rows], w_send.at[1, half],
-            w_recv.at[layer, half, j], section(1 + 2 * half),
-        )
-
-    def w_left(kind, way, n):
-        rows = pl.ds(0, n)
-        return remote(
-            w_hbm.at[0, rows], w_buf.at[s, rows], w_send.at[kind, way], w_recv.at[0, 0, 0],
-            section(1),
-        )
+            src, w_buf.at[layer, rows], w_send.at[way], w_recv.at[layer, j], section(1 + 2 * way)
+        )
+
+    def w_left(way, n):
+        while n:
+            now = min(n, WCH)
+            rows = pl.ds(0, now * WROWS)
+            remote(
+                w_buf.at[0, rows], w_buf.at[0, rows], w_send.at[way], w_recv.at[0, 0], section(1)
+            ).wait_send()
+            n -= now
 
     def sm_copy(d):
         return remote(sm_src.at[d], sm_buf.at[s], sm_send.at[d], sm_recv.at[d], section(d))
@@ -156,32 +195,35 @@
             cs_send.at[l, h, q], cs_recv.at[l, h, q], partner,
         )
 
-    def ce_copy(l, h):
-        return remote(
-            ce_src.at[l, h], ce_dst.at[l, h], ce_send.at[l, h], ce_recv.at[l, h], partner
-        )
+    def ce_copy(l):
+        return remote(ce_src.at[l], ce_dst.at[l], ce_send.at[l], ce_recv.at[l], partner)
 
     def rs_copy(l, h, p, g):
         return remote(
-            rs_src.at[l, h, p], rs_dst.at[l, h, p], rs_send.at[l, h], rs_recv.at[l, h, g], plane(p)
+            rs_src.at[l, h, p, pl.ds(0, RSB[h])], rs_dst.at[l, h, p, pl.ds(0, RSB[h])],
+            rs_send.at[l, h], rs_recv.at[l, h, g], plane(p),
         )
 
     def rs_all(l, h, first, n, g):
         part = pl.ds(first, n)
         return remote(
-            rs_src.at[l, h, part], rs_dst.at[l, h, part],
+            rs_src.at[l, h, part, pl.ds(0, RSB[h])], rs_dst.at[l, h, part, pl.ds(0, RSB[h])],
             rs_send.at[l, h], rs_recv.at[l, h, g], partner,
         )
 
-    def lx_copy():
-        return remote(lx_src, lx_dst, lx_send, lx_recv, partner)
-
-    def ex_copy(p):
-        return remote(ex_src, ex_dst.at[p], ex_send, ex_recv, plane(p))
-
-    def ex_all():
-        part = ex_dst.at[pl.ds(1, CHIPS - 1)]
-        return remote(part, part, ex_send, ex_recv, partner)
+    def lx_copy(first, n):
+        rows, k = pl.ds(first, n), int(first > 0)
+        return remote(lx_src.at[rows], lx_dst.at[rows], lx_send.at[k], lx_recv.at[k], partner)
+
+    def ex_copy(p, first, n):
+        rows, k = pl.ds(first, n), int(first > 0)
+        return remote(
+            ex_src.at[rows], ex_dst.at[p, rows], ex_send.at[k], ex_recv.at[k], plane(p)
+        )
+
+    def ex_all(first, n):
+        part, k = ex_dst.at[pl.ds(1, CHIPS - 1), pl.ds(first, n)], int(first > 0)
+        return remote(part, part, ex_send.at[k], ex_recv.at[k], partner)
 
     def od_copy(d):
         return remote(
@@ -190,6 +232,12 @@
 
     def group_of(p):
         return [g for g, (first, n) in enumerate(GROUPS) if first <= p < first + n][0]
+
+    barrier = pltpu.get_barrier_semaphore()
+    peers = [plane(p) for p in reversed(range(1, CHIPS))]
+    peers += [section(d) for d in (2, 1, 3)] + [partner]
+    for peer in peers:
+        pl.semaphore_signal(barrier, inc=1, device_id=peer, device_id_type=MESH)
 
     own_x = pltpu.make_async_copy(x_hbm.at[s], cur, loc_sem.at[0])
     own_x.start()
@@ -206,10 +254,6 @@
     own_g = pltpu.make_async_copy(g_hbm.at[s], grad, loc_sem.at[5])
     own_g.start()
 
-    barrier = pltpu.get_barrier_semaphore()
-    peers = [plane(p) for p in range(1, CHIPS)] + [section(d) for d in (1, 2, 3)] + [partner]
-    for peer in peers:
-        pl.semaphore_signal(barrier, inc=1, device_id=peer, device_id_type=MESH)
     own_a.wait()
     own_b.wait()
     own_m.wait()
@@ -237,24 +281,32 @@
             ag_copy(l, h, p, group_of(p)).start()
         cf_copy(l, h, 0, 1, 3, c).start()
 
-    def send_own(way):
-        for half in (way, 1 - way):
-            every(WCH, lambda j: w_own(way, half, j).start())
-
-    def pass_on(layer, half):
-        def one(j):
-            w_pass(layer, half, j).wait_recv()
-            w_pass(layer, half, j).start()
-
-        every(WCH, one)
-
-    @pl.when(s != 1)
-    def _():
-        send_own(0)
-
-    @pl.when(s != 3)
-    def _():
-        send_own(1)
+    def split_stage(k):
+        events = ROUTES[k][0]
+        n = 0
+        while n < len(events) and events[n][1] == k:
+            n += 1
+        return events[:n], events[n:]
+
+    def send_events(k, events):
+        for way, layer, first, n in events:
+
+            def one(j):
+                copy = w_copy(way, layer, first + j, layer == k)
+                if layer != k:
+                    copy.wait_recv()
+                copy.start()
+
+            every(n, one)
+
+    def in_section(fn):
+        for k in range(4):
+
+            @pl.when(s == k)
+            def _():
+                fn(k)
+
+    in_section(lambda k: send_events(k, split_stage(k)[0]))
 
     for h in range(NH):
         send_block(0, h)
@@ -266,38 +318,110 @@
     for p in reversed(range(1, CHIPS)):
         aa_copy(p, group_of(p)).start()
 
-    @pl.when(s == 1)
-    def _():
-        pass_on(0, 0)
-        send_own(0)
-        w_left(0, 1, D).wait_send()
-        pass_on(2, 1)
-
-    @pl.when(s == 3)
-    def _():
-        pass_on(0, 1)
-        send_own(1)
-        w_left(0, 0, D).wait_send()
-        pass_on(2, 0)
-
+    in_section(lambda k: send_events(k, split_stage(k)[1]))
     own_w.wait()
+    own_g.wait()
 
     for g, (first, n) in enumerate(GROUPS):
         aa_all(first, n, g).wait_recv()
     ac_copy(c).start()
     ac_copy(1 - c).wait_recv()
 
-    def pass_late():
-        @pl.when((s == 0) | (s == 2))
-        def _():
-            w_left(0, 0, D).wait_send()
-            w_left(0, 1, D).wait_send()
-            pass_on((s + 3) % 4, 0)
-            pass_on((s + 1) % 4, 1)
+    def weights_of(k, l):
+        if l:
+            send_events(k, ROUTES[k].get(l, []))
+        if l != k:
+            for first, n in awaited(k, l, l):
+                every(n, lambda j: w_copy(0, l, first + j, False).wait_recv())
 
     def a_rows(l, p):
         rows = pl.ds(pl.multiple_of(l * R, R), R)
         return jnp.concatenate([ag_a[0, p, rows, :], ag_a[1, p, rows, :]], axis=1)
+
+    def local_grads(l):
+        up = grad[...].astype(F32)
+        gm = jnp.sum(up * sv_branch[l], axis=0, keepdims=True) / sv_norm[l, 0:1]
+        res[l, R : 2 * R] = dot(sv_low[l], sv_gb[...], 0, 0)
+        res[l, 2 * R : 2 * R + 8] = jnp.broadcast_to(gm, (8, COLS))
+
+    def begin(l, h):
+        tokens = slice(h * H, (h + 1) * H)
+        branch = sv_branch[l, tokens]
+        b_l = sm_buf[l, R : 2 * R]
+        grad_branch = (grad[tokens].astype(F32) * sv_scale[l, 0:1]).astype(BF16)
+        sv_gb[tokens] = grad_branch
+        last = h == NH - 1
+        if last:
+            ce_src[l] = dot(b_l, sv_gb[...], 1, 1)
+            ce_copy(l).start()
+        rank = dot(grad_branch, b_l, 1, 1)
+        rank_hi = rank.astype(BF16)
+        rank_lo = (rank - rank_hi.astype(F32)).astype(BF16)
+        rank_two = jnp.concatenate([rank_hi, rank_lo], axis=1)
+        row = jnp.sum(grad_branch.astype(F32) * branch, axis=1, keepdims=True)
+        share = row * (1.0 / D) / sv_root[l, tokens]
+
+        def part(p):
+            q = inverse(p)
+            rows = w_buf[l, pl.ds(pl.multiple_of(source(q) * 256, 256), 256), :]
+            a_q = a_rows(l, q)
+            both = dot(grad_branch, rows, 1, 1) + dot(
+                rank_two, jnp.concatenate([a_q, a_q], axis=0), 1, 0
+            )
+            zero = both[:, 0:COLS] - xg[l, h, 0, q].astype(F32) * share
+            one = both[:, COLS:] - xg[l, h, 1, q].astype(F32) * share
+            return jnp.where(c == 0, one, zero), jnp.where(c == 0, zero, one)
+
+        def work(q):
+            for p in range(QUADS[q], QUADS[q] + 4):
+                theirs, mine = part(p)
+                cs_src[l, h, p] = theirs.astype(BF16)
+                mine_buf[p] = mine
+            cs_copy(l, h, q).start()
+
+        work(0)
+        work(1)
+        for q in range(4):
+            if q < 2:
+                work(q + 2)
+            if last and q == 0:
+                ce_copy(l).wait_recv()
+                ext = ce_src[l] + ce_dst[l]
+                own_ext[...] = ext
+                ext_b = ext.astype(BF16)
+            cs_copy(l, h, q).wait_recv()
+            for p in reversed(range(QUADS[q], QUADS[q] + 4)):
+                total = mine_buf[p] + cs_dst[l, h, p].astype(F32)
+                if p:
+                    rs_src[l, h, p, 0:H] = total.astype(BF16)
+                    if last:
+                        rs_src[l, h, p, H : H + R] = ext_b
+                    rs_copy(l, h, p, group_of(p)).start()
+                else:
+                    own_sum[h] = total
+        if last:
+            local_grads(l)
+
+    def normed_own(l):
+        x_own = jnp.concatenate([xg[l, i, c, 0] for i in range(NH)], axis=0)
+        return (x_own.astype(F32) / sv_root[l]).astype(BF16)
+
+    def adapter_grad(l, rank_sum):
+        res[l, 0:R] = fold3(dot(split3(rank_sum), normed_own(l), 1, 0))
+
+    def finish(l, h):
+        tokens = slice(h * H, (h + 1) * H)
+        total = own_sum[h]
+        rank_sum = own_ext[...]
+        for g, (first, n) in enumerate(GROUPS):
+            rs_all(l, h, first, n, g).wait_recv()
+            for p in range(first, first + n):
+                total = total + rs_dst[l, h, p, 0:H].astype(F32)
+                if h == NH - 1:
+                    rank_sum = rank_sum + rs_dst[l, h, p, H : H + R].astype(F32)
+        state = grad[tokens].astype(F32) + total / sv_root[l, tokens]
+        grad[tokens] = state.astype(BF16)
+        return rank_sum
 
     def w_rows(l, p):
         return w_buf[l, pl.ds(pl.multiple_of(source(p) * 256, 256), 256), :]
@@ -324,19 +448,11 @@
         sv_scale[l] = jnp.broadcast_to(mg_buf[l, 0:1] / norm, (8, COLS))
 
     def forward(l, _):
-        @pl.when(l == 1)
-        def _():
-            pass_late()
-
-        behind = (s + 4 - l) % 4
-
-        @pl.when(behind >= 2)
-        def _():
-            every(WCH, lambda j: w_pass(l, 0, j).wait_recv())
-
-        @pl.when((behind == 1) | (behind == 2))
-        def _():
-            every(WCH, lambda j: w_pass(l, 1, j).wait_recv())
+        for layer in range(L):
+
+            @pl.when(l == layer)
+            def _():
+                in_section(lambda k: weights_of(k, layer))
 
         column_norms(l)
         for h in range(NH):
@@ -379,138 +495,38 @@
             def _():
                 send_block(l + 1, h)
 
+            @pl.when(l == L - 1)
+            def _():
+                begin(L - 1, h)
+
         return 0
 
     lax.fori_loop(0, L, forward, 0)
-
-    own_g.wait()
-
-    def local_grads(l, h0, h1, first):
-        tokens = slice(h0, h1)
-        up = grad[tokens].astype(F32)
-        branch = sv_branch[l, tokens]
-        grad_branch = (up * sv_scale[l, 0:1]).astype(BF16)
-        gm = jnp.sum(up * branch, axis=0, keepdims=True) / sv_norm[l, 0:1]
-        gm = jnp.broadcast_to(gm, (8, COLS))
-        gb = dot(sv_low[l, tokens], grad_branch, 0, 0)
-        if not first:
-            gb = gb + res[l, R : 2 * R]
-            gm = gm + res[l, 2 * R : 2 * R + 8]
-        res[l, R : 2 * R] = gb
-        res[l, 2 * R : 2 * R + 8] = gm
-        rank_t = dot(sm_buf[l, R : 2 * R], grad_branch, 1, 1)
-        return branch, grad_branch, rank_t
-
-    def begin(l, h):
-        tokens = slice(h * H, (h + 1) * H)
-        branch, grad_branch, rank_t = local_grads(l, h * H, (h + 1) * H, h == 0)
-        prod = grad_branch.astype(F32) * branch * sv_root[l, tokens]
-        row = jnp.sum(prod.T, axis=0, keepdims=True)
-        row = jnp.concatenate([row, jnp.zeros((1, COLS - H), F32)], axis=1)
-        ce_src[l, h] = jnp.concatenate(
-            [
-                jnp.concatenate([rank_t[0:8], rank_t[8:16]], axis=1),
-                jnp.broadcast_to(row, (8, COLS)),
-            ],
-            axis=0,
-        )
-        ce_copy(l, h).start()
-        rank = rank_t.T
-        rank_hi = rank.astype(BF16)
-        rank_lo = (rank - rank_hi.astype(F32)).astype(BF16)
-        rank_two = jnp.concatenate([rank_hi, rank_lo], axis=1)
-
-        def part(p, core):
-            q = inverse(p)
-            start = pl.multiple_of(source(q) * 256 + core * COLS, COLS)
-            rows = w_buf[l, pl.ds(start, COLS), :]
-            a_q = ag_a[core, q, pl.ds(pl.multiple_of(l * R, R), R), :]
-            return dot(grad_branch, rows, 1, 1) + dot(
-                rank_two, jnp.concatenate([a_q, a_q], axis=0), 1, 0
-            )
-
-        def away(q):
-            for p in range(QUADS[q], QUADS[q] + 4):
-                cs_src[l, h, p] = part(p, 1 - c).astype(BF16)
-            cs_copy(l, h, q).start()
-
-        away(0)
-        away(1)
-        ext_b = None
-        for q in range(4):
-            if q < 2:
-                away(q + 2)
-            mine = {p: part(p, c) for p in range(QUADS[q], QUADS[q] + 4)}
-            if q == 0:
-                ce_copy(l, h).wait_recv()
-                ext = ce_src[l, h] + ce_dst[l, h]
-                row = ext[8:16, 0:H]
-                row_hi = row.astype(BF16).astype(F32)
-                ext = jnp.concatenate(
-                    [ext[0:8], jnp.concatenate([row_hi, row - row_hi], axis=1)], axis=0
-                )
-                own_ext[h] = ext
-                ext_b = ext.astype(BF16)
-            cs_copy(l, h, q).wait_recv()
-            for p in reversed(range(QUADS[q], QUADS[q] + 4)):
-                total = mine[p] + cs_dst[l, h, p].astype(F32)
-                if p:
-                    rs_src[l, h, p, 0:H] = total.astype(BF16)
-                    rs_src[l, h, p, H:RSB] = ext_b
-                    rs_copy(l, h, p, group_of(p)).start()
-                else:
-                    own_sum[h] = total
-
-    def adapter_grad(l, h0, h1, rank_sum, first):
-        tokens = slice(h0, h1)
-        if h1 - h0 == TOK:
-            x_own = jnp.concatenate([xg[l, i, c, 0] for i in range(NH)], axis=0)
-        else:
-            x_own = xg[l, h0 // H, c, 0]
-        normed = (x_own.astype(F32) / sv_root[l, tokens]).astype(BF16)
-        ga = fold3(dot(split3(rank_sum), normed, 1, 0))
-        if not first:
-            ga = ga + res[l, 0:R]
-        res[l, 0:R] = ga
-
-    def finish(l, h):
-        tokens = slice(h * H, (h + 1) * H)
-        total = jnp.concatenate([own_sum[h], own_ext[h]], axis=0)
-        for g, (first, n) in enumerate(GROUPS):
-            rs_all(l, h, first, n, g).wait_recv()
-            for p in range(first, first + n):
-                total = total + rs_dst[l, h, p].astype(F32)
-        grad_h = total[0:H]
-        rank = total[H : H + 8]
-        rank_sum = jnp.concatenate([rank[:, 0:H], rank[:, H:]], axis=0)
-        row = total[H + 8 : H + 9]
-        row = row[:, 0:H] + row[:, H:]
-        row_dot = jnp.broadcast_to(row, (COLS, H)).T
-        up = grad[tokens].astype(F32)
-        x_own = xg[l, h, c, 0].astype(F32)
-        inv = 1.0 / sv_root[l, tokens]
-        state = up + (grad_h - x_own * (row_dot * (inv * inv) * (1.0 / D))) * inv
-        grad[tokens] = state.astype(BF16)
-        return rank_sum
-
-    for h in range(NH):
-        begin(L - 1, h)
 
     def backward(i, _):
         l = L - 1 - i
         for h in range(NH):
             rank_sum = finish(l, h)
+            if h == NH - 1:
+                rank_buf[...] = rank_sum
 
             @pl.when(l > 1)
             def _():
                 begin(l - 1, h)
 
-            adapter_grad(l, h * H, (h + 1) * H, rank_sum, h == 0)
+        @pl.when(l > 1)
+        def _():
+            adapter_grad(l, rank_buf[...])
+
         return 0
 
     lax.fori_loop(0, L - 1, backward, 0)
 
-    _, _, rank_t = local_grads(0, 0, TOK, True)
+    sv_gb[...] = (grad[...].astype(F32) * sv_scale[0, 0:1]).astype(BF16)
+    lx_src[0:R] = dot(sm_buf[0, R : 2 * R], sv_gb[...], 1, 1)
+    lx_copy(0, R).start()
+    adapter_grad(1, rank_buf[...])
+    local_grads(0)
     sum_a = jnp.zeros((1, COLS), F32)
     sum_b = jnp.zeros((1, COLS), F32)
     sum_m = jnp.zeros((1, COLS), F32)
@@ -522,15 +538,19 @@
         sum_b = sum_b + jnp.sum(gb * gb, axis=0, keepdims=True)
         gm = res[l, 2 * R : 2 * R + 1]
         sum_m = sum_m + gm * gm
-    lx_src[...] = jnp.concatenate(
-        [rank_t, sum_a, sum_b, sum_m, jnp.zeros((5, COLS), F32)], axis=0
-    )
-    lx_copy().start()
-    lx_copy().wait_recv()
-    ext = lx_src[...] + lx_dst[...]
-    ex_src[...] = ext
+    lx_src[R : R + 8] = jnp.concatenate([sum_a, sum_b, sum_m, jnp.zeros((5, COLS), F32)], axis=0)
+    lx_copy(R, 8).start()
+    lx_copy(0, R).wait_recv()
+    rank_sum = lx_src[0:R] + lx_dst[0:R]
+    ex_src[0:R] = rank_sum
     for p in reversed(range(1, CHIPS)):
-        ex_copy(p).start()
+        ex_copy(p, 0, R).start()
+    lx_copy(R, 8).wait_recv()
+    sums = lx_src[R : R + 8] + lx_dst[R : R + 8]
+    ex_src[R : R + 8] = sums
+    for p in reversed(range(1, CHIPS)):
+        ex_copy(p, R, 8).start()
+    normed = normed_own(0)
     outer = jnp.zeros((TOK, TOK), F32)
     for p in range(CHIPS):
         both = jnp.concatenate(
@@ -543,19 +563,25 @@
         outer = outer + dot(both, both, 1, 1)
     inv = 1.0 / sv_root[0]
     outer = outer * inv * inv.T
-    ex_all().wait_recv()
+    outer_hi = outer.astype(BF16)
+    outer_lo = (outer - outer_hi.astype(F32)).astype(BF16)
+    right = jnp.concatenate([normed, outer_hi, outer_lo], axis=1)
+    ex_all(R, 8).wait_recv()
     for p in range(1, CHIPS):
-        ext = ext + ex_dst[p]
-    rank_sum = ext[0:R]
-    adapter_grad(0, 0, TOK, rank_sum, True)
-    sq = rank_sum * dot(rank_sum, outer, 1, 0, HIGHEST)
+        sums = sums + ex_dst[p, R : R + 8]
+    ex_all(0, R).wait_recv()
+    for p in range(1, CHIPS):
+        rank_sum = rank_sum + ex_dst[p, 0:R]
+    made = fold3(dot(split3(rank_sum), right, 1, 0))
+    res[0, 0:R] = made[:, 0:COLS]
+    sq = rank_sum * (made[:, COLS : 2 * COLS] + made[:, 2 * COLS :])
 
     def norm_of(v, count):
         return 1.0 / jnp.sqrt(jnp.sum(v, axis=1, keepdims=True) * (1.0 / count) + 1e-06)
 
-    by_a = norm_of(ext[R : R + 1] + jnp.sum(sq, axis=0, keepdims=True), L * R * D)
-    by_b = norm_of(ext[R + 1 : R + 2], L * R * D)
-    by_m = norm_of(ext[R + 2 : R + 3], L * D)
+    by_a = norm_of(sums[0:1] + jnp.sum(sq, axis=0, keepdims=True), L * R * D)
+    by_b = norm_of(sums[1:2], L * R * D)
+    by_m = norm_of(sums[2:3], L * D)
     for l in range(L):
         od_src[l, 0:R] = res[l, 0:R] * by_a
         od_src[l, R : 2 * R] = res[l, R : 2 * R] * by_b
@@ -564,16 +590,11 @@
         od_copy(d).start()
     od_dst[s] = od_src[s]
 
-    @pl.when(s == 1)
-    def _():
-        w_left(0, 0, D).wait_send()
-
-    @pl.when(s == 3)
-    def _():
-        w_left(0, 1, D).wait_send()
-
-    w_left(1, 0, HALF).wait_send()
-    w_left(1, 1, HALF).wait_send()
+    def drain_w(k):
+        for way in range(2):
+            w_left(way, sent(k, way))
+
+    in_section(drain_w)
     aa_all(1, CHIPS - 1, 0).wait_send()
     ac_copy(c).wait_send()
 
@@ -590,13 +611,15 @@
         l = i + 1
         for h in range(NH):
             rs_all(l, h, 1, CHIPS - 1, 0).wait_send()
-            ce_copy(l, h).wait_send()
             for q in range(4):
                 cs_copy(l, h, q).wait_send()
+        ce_copy(l).wait_send()
 
     every(L - 1, drain_b)
-    lx_copy().wait_send()
-    ex_all().wait_send()
+    lx_copy(0, R).wait_send()
+    lx_copy(R, 8).wait_send()
+    ex_all(0, R).wait_send()
+    ex_all(R, 8).wait_send()
     for d in range(1, 4):
         sm_copy(d).wait_send()
         mg_copy(d).wait_send()
@@ -645,14 +668,17 @@
             pltpu.VMEM((L, TOK, COLS), F32),
             pltpu.VMEM((L, 8, COLS), F32),
             pltpu.VMEM((L, 8, COLS), F32),
+            pltpu.VMEM((TOK, COLS), BF16),
+            pltpu.VMEM((CHIPS, H, COLS), F32),
             pltpu.VMEM((L, NH, CHIPS, H, COLS), BF16),
             pltpu.VMEM((L, NH, CHIPS, H, COLS), BF16),
-            pltpu.VMEM((L, NH, EXT, COLS), F32),
-            pltpu.VMEM((L, NH, EXT, COLS), F32),
-            pltpu.VMEM((L, NH, CHIPS, RSB, COLS), BF16),
-            pltpu.VMEM((L, NH, CHIPS, RSB, COLS), BF16),
+            pltpu.VMEM((L, R, TOK), F32),
+            pltpu.VMEM((L, R, TOK), F32),
+            pltpu.VMEM((L, NH, CHIPS, H + R, COLS), BF16),
+            pltpu.VMEM((L, NH, CHIPS, H + R, COLS), BF16),
             pltpu.VMEM((NH, H, COLS), F32),
-            pltpu.VMEM((NH, EXT, COLS), F32),
+            pltpu.VMEM((R, TOK), F32),
+            pltpu.VMEM((R, TOK), F32),
             pltpu.VMEM((R + 8, TOK), F32),
             pltpu.VMEM((R + 8, TOK), F32),
             pltpu.VMEM((R + 8, TOK), F32),
@@ -661,8 +687,8 @@
             pltpu.VMEM((L, 2 * R + 8, COLS), F32),
             pltpu.VMEM((L, 2 * R + 8, COLS), F32),
             dma((6,)),
-            dma((2, 2)),
-            dma((L, 2, WCH)),
+            dma((2,)),
+            dma((L, WCH)),
             dma((4,)),
             dma((4,)),
             dma((4,)),
@@ -677,14 +703,14 @@
             dma((L, NH, 4)),
             dma((L, NH, 4)),
             dma((L, NH, 4)),
-            dma((L, NH)),
-            dma((L, NH)),
+            dma((L,)),
+            dma((L,)),
             dma((L, NH)),
             dma((L, NH, 3)),
-            dma,
-            dma,
-            dma,
-            dma,
+            dma((2,)),
+            dma((2,)),
+            dma((2,)),
+            dma((2,)),
             dma((4,)),
             dma((4,)),
         ],

time: 118 us -> 113 us (0.958)
  Pallas kernels: 114 us -> 109 us
    pallas_call x1, Pallas kernels: 114 us -> 109 us  [local(): pl.pallas_call(kernel, out_shape=(jax.ShapeDtypeStruct((1, 4, R, COLS), F...]
where the time goes in v4:
time: 113 us
  Pallas kernels  109 us (96%)
  local copies, waits for them, and re-layouts  2.64 us (2%)
    pallas_call x1, Pallas kernels, local(): pl.pallas_call(kernel, out_shape=(jax.ShapeDtypeStruct((1, 4, R, COLS), F...  109 us
    unnamed x7, local copies, waits for them, and re-layouts  2.64 us

profile of v4, /device:TPU:0, one launch (start us, length us, event | category | flops | bytes accessed | tf_op | source)
XLA Modules:
  0.0 112.5 jit_solution(5981389566550390875)
XLA Ops:
  0.6 109.2 %shard_map.94 = (f32[1,4,16,128]{3,2,1,0:T(8,128)}, f32[1,4,16,128]{3,2,1,0:T(8,128)}, f32[1,4,128]{2,1,0:T(4,128)}) custom-call(s32[4]{0:T(128)} %ten_ref.1, bf16[4,128,128]{2,1,0:T(8,128)(2,1)} %x_hbm.1, bf16[4,128,128]{2,1,0:T(8,128)(2,1)} %g_hbm.1, bf16[1,4096,128]{2,1,0:T(8,128)(2,1)} %w_hbm.1, bf16[1,4,16,4096]{3,2,1,0:T(8,128)(2,1)} %a_hbm.1, ...), custom_call_target="tpu_custom_call" | custom-call | tf_op jit(solution)/shard_map/pallas_call | solution.py:644
  109.9 0.0 copy-start
  109.9 1.4 %copy.13 = f32[1,4,16,128]{3,2,1,0:T(8,128)} copy(f32[1,4,16,128]{3,2,1,0:T(8,128)} %get-tuple-element.6) | data formatting | bytes 65536
  111.3 0.0 copy-done
  111.3 0.0 copy-start.1
  111.3 0.6 copy.14
  111.9 0.1 copy-done.1
  111.9 0.6 copy.15
Async XLA Ops:
  109.9 1.4 %copy-start = (f32[1,4,16,128]{3,2,1,0:T(8,128)S(1)}, f32[1,4,16,128]{3,2,1,0:T(8,128)}, u32[]{:S(2)}) copy-start(f32[1,4,16,128]{3,2,1,0:T(8,128)} %get-tuple-element.7) | copy-start | bytes 98308
  111.3 0.7 copy-start.1

commit v5 on v4

--- a/solution.py
+++ b/solution.py
@@ -75,8 +75,9 @@
 
 
 NEAR = sorted(range(CHIPS), key=hops)
-GROUPS = [(1, 4), (5, 6), (11, 5)]
-QUADS = [12, 8, 4, 0]
+GROUPS = [(1, 4), (5, 11)]
+RS_GROUPS = [(1, 4), (5, 11)]
+RUNS = [8, 0]
 
 
 def inverse(p):
@@ -189,7 +190,7 @@
         return remote(part, part, cf_send.at[l, h, g], cf_recv.at[l, h, g], partner)
 
     def cs_copy(l, h, q):
-        part = pl.ds(QUADS[q], 4)
+        part = pl.ds(RUNS[q], 8)
         return remote(
             cs_src.at[l, h, part], cs_dst.at[l, h, part],
             cs_send.at[l, h, q], cs_recv.at[l, h, q], partner,
@@ -230,8 +231,8 @@
             od_src.at[(s + d) % 4], od_dst.at[s], od_send.at[d], od_recv.at[d], section(d)
         )
 
-    def group_of(p):
-        return [g for g, (first, n) in enumerate(GROUPS) if first <= p < first + n][0]
+    def group_of(p, groups=GROUPS):
+        return [g for g, (first, n) in enumerate(groups) if first <= p < first + n][0]
 
     barrier = pltpu.get_barrier_semaphore()
     peers = [plane(p) for p in reversed(range(1, CHIPS))]
@@ -279,7 +280,7 @@
         xg[l, h, c, 0] = cur[h * H : (h + 1) * H]
         for p in reversed(range(1, CHIPS)):
             ag_copy(l, h, p, group_of(p)).start()
-        cf_copy(l, h, 0, 1, 3, c).start()
+        cf_copy(l, h, 0, 1, 2, c).start()
 
     def split_stage(k):
         events = ROUTES[k][0]
@@ -373,7 +374,7 @@
             return jnp.where(c == 0, one, zero), jnp.where(c == 0, zero, one)
 
         def work(q):
-            for p in range(QUADS[q], QUADS[q] + 4):
+            for p in range(RUNS[q], RUNS[q] + 8):
                 theirs, mine = part(p)
                 cs_src[l, h, p] = theirs.astype(BF16)
                 mine_buf[p] = mine
@@ -381,22 +382,20 @@
 
         work(0)
         work(1)
-        for q in range(4):
-            if q < 2:
-                work(q + 2)
+        for q in range(2):
             if last and q == 0:
                 ce_copy(l).wait_recv()
                 ext = ce_src[l] + ce_dst[l]
                 own_ext[...] = ext
                 ext_b = ext.astype(BF16)
             cs_copy(l, h, q).wait_recv()
-            for p in reversed(range(QUADS[q], QUADS[q] + 4)):
+            for p in reversed(range(RUNS[q], RUNS[q] + 8)):
                 total = mine_buf[p] + cs_dst[l, h, p].astype(F32)
                 if p:
                     rs_src[l, h, p, 0:H] = total.astype(BF16)
                     if last:
                         rs_src[l, h, p, H : H + R] = ext_b
-                    rs_copy(l, h, p, group_of(p)).start()
+                    rs_copy(l, h, p, group_of(p, RS_GROUPS)).start()
                 else:
                     own_sum[h] = total
         if last:
@@ -413,7 +412,7 @@
         tokens = slice(h * H, (h + 1) * H)
         total = own_sum[h]
         rank_sum = own_ext[...]
-        for g, (first, n) in enumerate(GROUPS):
+        for g, (first, n) in enumerate(RS_GROUPS):
             rs_all(l, h, first, n, g).wait_recv()
             for p in range(first, first + n):
                 total = total + rs_dst[l, h, p, 0:H].astype(F32)
@@ -472,7 +471,7 @@
                     ssq = ssq + wide[:, 0:COLS] + wide[:, COLS:]
                 return acc, low_acc, ssq
 
-            before = (0, 1, 3)
+            before = (0, 1, 2)
             for g, (first, n) in enumerate(GROUPS):
                 ag_all(l, h, first, n, g).wait_recv()
                 cf_copy(l, h, first, n, g, c).start()
@@ -601,7 +600,7 @@
     def drain_l(l):
         for h in range(NH):
             ag_all(l, h, 1, CHIPS - 1, 0).wait_send()
-            cf_copy(l, h, 0, 1, 3, c).wait_send()
+            cf_copy(l, h, 0, 1, 2, c).wait_send()
             for g, (first, n) in enumerate(GROUPS):
                 cf_copy(l, h, first, n, g, c).wait_send()
 
@@ -611,7 +610,7 @@
         l = i + 1
         for h in range(NH):
             rs_all(l, h, 1, CHIPS - 1, 0).wait_send()
-            for q in range(4):
+            for q in range(2):
                 cs_copy(l, h, q).wait_send()
         ce_copy(l).wait_send()
 

time: 113 us -> 105 us (0.929)
  Pallas kernels: 109 us -> 101 us
    pallas_call x1, Pallas kernels: 109 us -> 101 us  [local(): pl.pallas_call(kernel, out_shape=(jax.ShapeDtypeStruct((1, 4, R, COLS), F...]
where the time goes in v5:
time: 105 us
  Pallas kernels  101 us (96%)
  local copies, waits for them, and re-layouts  2.64 us (3%)
    pallas_call x1, Pallas kernels, local(): pl.pallas_call(kernel, out_shape=(jax.ShapeDtypeStruct((1, 4, R, COLS), F...  101 us
    unnamed x7, local copies, waits for them, and re-layouts  2.64 us

profile of v5, /device:TPU:0, one launch (start us, length us, event | category | flops | bytes accessed | tf_op | source)
XLA Modules:
  0.0 104.7 jit_solution(4038038494893418315)
XLA Ops:
  0.6 101.4 %shard_map.94 = (f32[1,4,16,128]{3,2,1,0:T(8,128)}, f32[1,4,16,128]{3,2,1,0:T(8,128)}, f32[1,4,128]{2,1,0:T(4,128)}) custom-call(s32[4]{0:T(128)} %ten_ref.1, bf16[4,128,128]{2,1,0:T(8,128)(2,1)} %x_hbm.1, bf16[4,128,128]{2,1,0:T(8,128)(2,1)} %g_hbm.1, bf16[1,4096,128]{2,1,0:T(8,128)(2,1)} %w_hbm.1, bf16[1,4,16,4096]{3,2,1,0:T(8,128)(2,1)} %a_hbm.1, ...), custom_call_target="tpu_custom_call" | custom-call | tf_op jit(solution)/shard_map/pallas_call | solution.py:643
  102.0 0.0 copy-start
  102.1 1.4 %copy.13 = f32[1,4,16,128]{3,2,1,0:T(8,128)} copy(f32[1,4,16,128]{3,2,1,0:T(8,128)} %get-tuple-element.6) | data formatting | bytes 65536
  103.4 0.0 copy-done
  103.4 0.0 copy-start.1
  103.4 0.6 copy.14
  104.1 0.1 copy-done.1
  104.1 0.6 copy.15
Async XLA Ops:
  102.0 1.4 %copy-start = (f32[1,4,16,128]{3,2,1,0:T(8,128)S(1)}, f32[1,4,16,128]{3,2,1,0:T(8,128)}, u32[]{:S(2)}) copy-start(f32[1,4,16,128]{3,2,1,0:T(8,128)} %get-tuple-element.7) | copy-start | bytes 98308
  103.4 0.7 copy-start.1

commit v6 on v5

--- a/solution.py
+++ b/solution.py
@@ -425,7 +425,14 @@
     def w_rows(l, p):
         return w_buf[l, pl.ds(pl.multiple_of(source(p) * 256, 256), 256), :]
 
-    def column_norms(l):
+    def adapter_part(l):
+        gram = jnp.zeros((R, R), F32)
+        for p in range(CHIPS):
+            a_p = a_rows(l, p)
+            gram = gram + dot(a_p, a_p, 1, 1)
+        return dot(gram, sm_buf[l, R : 2 * R].astype(F32), 1, 0, HIGHEST)
+
+    def column_norms(l, quad):
         def squares(i, total):
             rows = w_buf[l, pl.ds(pl.multiple_of(i * 256, 256), 256), :].astype(F32)
             return total + jnp.sum((rows * rows).reshape(32, 8, COLS), axis=0)
@@ -434,26 +441,23 @@
             lax.fori_loop(0, 16, squares, jnp.zeros((8, COLS), F32)), axis=0, keepdims=True
         )
         cross = jnp.zeros((R, COLS), F32)
-        gram = jnp.zeros((R, R), F32)
         for p in range(CHIPS):
-            a_p = a_rows(l, p)
-            cross = cross + dot(a_p, w_rows(l, p), 1, 0)
-            gram = gram + dot(a_p, a_p, 1, 1)
+            cross = cross + dot(a_rows(l, p), w_rows(l, p), 1, 0)
         b_wide = sm_buf[l, R : 2 * R].astype(F32)
-        quad = dot(gram, b_wide, 1, 0, HIGHEST)
         total = base_sq + jnp.sum(b_wide * (2.0 * cross + quad), axis=0, keepdims=True)
         norm = jnp.sqrt(total + 1e-06)
         sv_norm[l] = jnp.broadcast_to(norm, (8, COLS))
         sv_scale[l] = jnp.broadcast_to(mg_buf[l, 0:1] / norm, (8, COLS))
 
     def forward(l, _):
+        quad = adapter_part(l)
         for layer in range(L):
 
             @pl.when(l == layer)
             def _():
                 in_section(lambda k: weights_of(k, layer))
 
-        column_norms(l)
+        column_norms(l, quad)
         for h in range(NH):
             tokens = slice(h * H, (h + 1) * H)
             acc = jnp.zeros((H, COLS), F32)

time: 105 us -> 105 us (level)
  no operation moved by 1% of the time
where the time goes in v6:
time: 105 us
  Pallas kernels  101 us (96%)
  local copies, waits for them, and re-layouts  2.64 us (3%)
    pallas_call x1, Pallas kernels, local(): pl.pallas_call(kernel, out_shape=(jax.ShapeDtypeStruct((1, 4, R, COLS), F...  101 us
    unnamed x7, local copies, waits for them, and re-layouts  2.64 us

profile of v6, /device:TPU:0, one launch (start us, length us, event | category | flops | bytes accessed | tf_op | source)
XLA Modules:
  0.0 104.8 jit_solution(7623203832788567493)
XLA Ops:
  0.6 101.5 %shard_map.94 = (f32[1,4,16,128]{3,2,1,0:T(8,128)}, f32[1,4,16,128]{3,2,1,0:T(8,128)}, f32[1,4,128]{2,1,0:T(4,128)}) custom-call(s32[4]{0:T(128)} %ten_ref.1, bf16[4,128,128]{2,1,0:T(8,128)(2,1)} %x_hbm.1, bf16[4,128,128]{2,1,0:T(8,128)(2,1)} %g_hbm.1, bf16[1,4096,128]{2,1,0:T(8,128)(2,1)} %w_hbm.1, bf16[1,4,16,4096]{3,2,1,0:T(8,128)(2,1)} %a_hbm.1, ...), custom_call_target="tpu_custom_call" | custom-call | tf_op jit(solution)/shard_map/pallas_call | solution.py:647
  102.1 0.0 copy-start
  102.1 1.4 %copy.13 = f32[1,4,16,128]{3,2,1,0:T(8,128)} copy(f32[1,4,16,128]{3,2,1,0:T(8,128)} %get-tuple-element.6) | data formatting | bytes 65536
  103.5 0.0 copy-done
  103.5 0.0 copy-start.1
  103.5 0.6 copy.14
  104.1 0.1 copy-done.1
  104.2 0.6 copy.15
Async XLA Ops:
  102.1 1.4 %copy-start = (f32[1,4,16,128]{3,2,1,0:T(8,128)S(1)}, f32[1,4,16,128]{3,2,1,0:T(8,128)}, u32[]{:S(2)}) copy-start(f32[1,4,16,128]{3,2,1,0:T(8,128)} %get-tuple-element.7) | copy-start | bytes 98308
  103.5 0.7 copy-start.1
